TPU v7x, 32 devices: a whole 2x2x4 slice. The times are simulated.
32 devices in a mesh: dp: 4 (over x, core), ctx: 8 (over z, y).
Axes of the slice: x: 2, y: 2, z: 4, core: 2. Of those that a mesh axis runs over, the one named last changes fastest.
Arguments:
- queries: bfloat16 [4096, 4096], P(('dp', 'ctx')), may hold values from -10 to 10
- keys: bfloat16 [4096, 4096], P(('dp', 'ctx')), may hold values from -10 to 10
- values: bfloat16 [4096, 4096], P(('dp', 'ctx')), may hold values from -6 to 6
- residual_in: bfloat16 [4096, 7168], P(('dp', 'ctx')), may hold values from -40 to 40
- out_weight: bfloat16 [4096, 7168], P('ctx', 'dp'), may hold values from -1.25 to 1.25
- norm_gain: float32 [7168], replicated, may hold values from 0.5 to 1.5
- norm_bias: float32 [7168], replicated, may hold values from -3 to 3
Outputs:
- layer_out: bfloat16 [4096, 7168], P(('dp', 'ctx'))
All inputs are finite; a program needn't handle non-finite values.
Results may differ from a plain program's by a relative error of at most 0.0085.
Values may be sent and summed in bfloat16 or wider, within the bound.
A program may use at most 128 MiB of HBM per device.

v0:
```python
import math

import jax
import jax.numpy as jnp
from jax import lax
from jax.sharding import PartitionSpec as P

HEADS = 32


deepnorm_alpha = 96.0**0.25
norm_eps = 1e-05


def block_rows(length):
    block = min(512, length)
    while length % block != 0:
        block = block + 1
    return block


def attend(all_queries, all_keys, all_values, local_heads):
    length = all_queries.shape[0]
    width = all_queries.shape[1]
    head_dim = width // local_heads
    block = block_rows(length)
    blocks = length // block
    scale = 1.0 / math.sqrt(head_dim)
    query_blocks = all_queries.reshape(blocks, block, local_heads, head_dim)
    key_heads = all_keys.reshape(length, local_heads, head_dim)
    value_heads = all_values.reshape(length, local_heads, head_dim)
    key_position = jnp.arange(length)

    def one_block(inputs):
        number, query_part = inputs
        scores = (
            jnp.einsum("qhd,khd->hqk", query_part, key_heads, preferred_element_type=jnp.float32)
            * scale
        )
        query_position = number * block + jnp.arange(block)
        causal = query_position[:, None] >= key_position[None, :]
        scores = jnp.where(causal[None], scores, -1e30)
        highest = jnp.max(scores, axis=-1, keepdims=True)
        expo = jnp.exp(scores - highest)
        probs = (expo / jnp.sum(expo, axis=-1, keepdims=True)).astype(jnp.bfloat16)
        result = jnp.einsum("hqk,khd->qhd", probs, value_heads, preferred_element_type=jnp.float32)
        return result.astype(jnp.bfloat16).reshape(block, width)

    outputs = lax.map(one_block, (jnp.arange(blocks), query_blocks))
    return outputs.reshape(length, width)


def local(queries, keys, values, residual_in, out_weight, norm_gain, norm_bias):
    head_q, head_k, head_v = (
        lax.all_to_all(queries, "ctx", split_axis=1, concat_axis=0, tiled=True),
        lax.all_to_all(keys, "ctx", split_axis=1, concat_axis=0, tiled=True),
        lax.all_to_all(values, "ctx", split_axis=1, concat_axis=0, tiled=True),
    )
    groups = lax.axis_size("ctx")
    attn_heads = attend(head_q, head_k, head_v, HEADS // groups)
    group_rows = lax.all_gather(out_weight, "dp", axis=1, tiled=True)
    summed = lax.psum_scatter(
        jnp.dot(attn_heads, group_rows, preferred_element_type=jnp.float32).astype(jnp.bfloat16),
        "ctx",
        scatter_dimension=0,
        tiled=True,
    )
    attn_float = lax.optimization_barrier(summed).astype(jnp.float32)
    mixed = deepnorm_alpha * residual_in.astype(jnp.float32) + attn_float
    mean = jnp.mean(mixed, axis=-1, keepdims=True)
    centered = mixed - mean
    var = jnp.mean(centered * centered, axis=-1, keepdims=True)
    normed = centered * lax.rsqrt(var + norm_eps) * norm_gain + norm_bias
    return normed.astype(jnp.bfloat16)


def solution(mesh):
    in_specs = (
        P(("dp", "ctx"), None),
        P(("dp", "ctx"), None),
        P(("dp", "ctx"), None),
        P(("dp", "ctx"), None),
        P("ctx", "dp"),
        P(),
        P(),
    )
    out_specs = P(("dp", "ctx"), None)
    return jax.shard_map(local, mesh=mesh, in_specs=in_specs, out_specs=out_specs, check_vma=False)
```

profile of v0, /device:TPU:0, one launch (start us, length us, event | category | flops | bytes accessed | tf_op | source)
XLA Modules:
  0.0 393.3 jit_solution(1607471463144156225)
XLA Ops:
  7.3 2.3 copy.46
  9.6 7.3 %all-to-all-start = ((bf16[128,8,512]{2,0,1:T(8,128)(2,1)}), bf16[128,8,512]{2,0,1:T(8,128)(2,1)S(1)}, u32[]{:S(2)}, u32[]{:S(2)}) async-start(bf16[128,8,512]{2,0,1:T(8,128)(2,1)} %bitcast.34), calls=%async_computation | async-start | bytes 2097152 | tf_op jit(solution)/shard_map/all_to_all | solution.py:55
  16.8 1.3 copy.23
  18.2 24.4 %all-to-all-done = bf16[128,8,512]{2,0,1:T(8,128)(2,1)S(1)} async-done(((bf16[128,8,512]{2,0,1:T(8,128)(2,1)}), bf16[128,8,512]{2,0,1:T(8,128)(2,1)S(1)}, u32[]{:S(2)}, u32[]{:S(2)}) %all-to-all-start) | async-done | bytes 1048608 | tf_op jit(solution)/shard_map/all_to_all | solution.py:55
  42.6 3.6 all-to-all-start.1
  46.2 2.3 copy.25
  48.5 23.7 %all-to-all-done.1 = bf16[128,8,512]{0,2,1:T(8,128)(2,1)S(1)} async-done(((bf16[128,8,512]{0,2,1:T(8,128)(2,1)}), bf16[128,8,512]{0,2,1:T(8,128)(2,1)S(1)}, u32[]{:S(2)}, u32[]{:S(2)}) %all-to-all-start.1) | async-done | bytes 1048608 | tf_op jit(solution)/shard_map/all_to_all | solution.py:56
  72.1 4.2 %all-to-all-start.2 = ((bf16[128,8,512]{0,2,1:T(8,128)(2,1)}), bf16[128,8,512]{0,2,1:T(8,128)(2,1)}, u32[]{:S(2)}, u32[]{:S(2)}) async-start(bf16[128,8,512]{0,2,1:T(8,128)(2,1)} %bitcast.3), calls=%async_computation.2 | async-start | bytes 2097152 | tf_op jit(solution)/shard_map/all_to_all | solution.py:57
  77.9 1.3 copy.28
  79.2 22.8 %all-to-all-done.2 = bf16[128,8,512]{0,2,1:T(8,128)(2,1)} async-done(((bf16[128,8,512]{0,2,1:T(8,128)(2,1)}), bf16[128,8,512]{0,2,1:T(8,128)(2,1)}, u32[]{:S(2)}, u32[]{:S(2)}) %all-to-all-start.2) | async-done | bytes 1048608 | tf_op jit(solution)/shard_map/all_to_all | solution.py:57
  102.0 1.9 copy.26
  103.9 1.3 reshape.78
  105.2 26.8 %while.11 = (s32[]{:T(128)}, bf16[2,512,512]{2,1,0:T(8,128)(2,1)}, s32[2]{0:T(128)S(1)}, bf16[2,512,4,128]{3,2,1,0:T(4,128)(2,1)S(1)}, bf16[1024,4,128]{2,0,1:T(...) while((s32[]{:T(128)}, bf16[2,512,512]{2,1,0:T(8,128)(2,1)}, ...), condition=%wide.region_3.4_spmd.clone, body=%wide.region_0.3_spmd.clone.sunk | while | flops 1087112704 | bytes 24137856 | solution.py:49
  107.0 5.4 %fusion.27 = (f32[4,512]{1,0:T(4,128)S(1)}, f32[4,512,1024]{2,1,0:T(8,128)}) fusion(pred[512,1024]{1,0:T(8,128)(4,1)S(1)} %iota_compare_fusion.2, bf16[1024,4,128]{2,0,1:T(8,128)(2,1)S(1)} %get-tuple-element.150, bf16[1,512,4,128]{3,2,1,0:T(4,128)(2,1)S(1)} %constant_dynamic-slice_fusion.2), kind=kOutput, calls=%fused_computation.28.clone.1 | convolution fusion | flops 545260544 | bytes 10493952 | tf_op jit(solution)/shard_map/while/body/eval_jaxpr/sub | solution.py:44
  112.4 5.2 %fusion.28 = bf16[4,512,128]{1,2,0:T(8,128)(2,1)S(1)} fusion(bf16[1024,4,128]{0,2,1:T(8,128)(2,1)} %get-tuple-element.151, f32[4,512,1024]{2,1,0:T(8,128)} %get-tuple-element.128, f32[4,512]{1,0:T(4,128)S(1)} %get-tuple-element.129), kind=kOutput, calls=%fused_computation.11.clone.1 | convolution fusion | flops 541327360 | bytes 9969664 | tf_op jit(solution)/shard_map/while/body/eval_jaxpr/hqk,khd->qhd/dot_general | solution.py:46
  117.8 0.8 constant_dynamic-update-slice_fusion.2
  120.4 5.4 %fusion.27 = (f32[4,512]{1,0:T(4,128)S(1)}, f32[4,512,1024]{2,1,0:T(8,128)}) fusion(pred[512,1024]{1,0:T(8,128)(4,1)S(1)} %iota_compare_fusion.2, bf16[1024,4,128]{2,0,1:T(8,128)(2,1)S(1)} %get-tuple-element.150, bf16[1,512,4,128]{3,2,1,0:T(4,128)(2,1)S(1)} %constant_dynamic-slice_fusion.2), kind=kOutput, calls=%fused_computation.28.clone.1 | convolution fusion | flops 545260544 | bytes 10493952 | tf_op jit(solution)/shard_map/while/body/eval_jaxpr/sub | solution.py:44
  125.8 5.2 %fusion.28 = bf16[4,512,128]{1,2,0:T(8,128)(2,1)S(1)} fusion(bf16[1024,4,128]{0,2,1:T(8,128)(2,1)} %get-tuple-element.151, f32[4,512,1024]{2,1,0:T(8,128)} %get-tuple-element.128, f32[4,512]{1,0:T(4,128)S(1)} %get-tuple-element.129), kind=kOutput, calls=%fused_computation.11.clone.1 | convolution fusion | flops 541327360 | bytes 9969664 | tf_op jit(solution)/shard_map/while/body/eval_jaxpr/hqk,khd->qhd/dot_general | solution.py:46
  131.2 0.8 constant_dynamic-update-slice_fusion.2
  132.1 13.3 %convolution_convert_fusion = bf16[1024,7168]{1,0:T(8,128)(2,1)} fusion(bf16[1024,512]{1,0:T(8,128)(2,1)} %bitcast.49, bf16[512,7168]{1,0:T(8,128)(2,1)} %all-gather.2.cloned.1.call-done), kind=kOutput, calls=%fused_computation.20 | convolution fusion | flops 7523532800 | bytes 23068672 | tf_op jit(solution)/shard_map/dot_general | solution.py:63
  145.4 235.5 %reduce-scatter.2.cloned.1.call-done = bf16[128,7168]{1,0:T(8,128)(2,1)} async-done(((bf16[1024,7168]{1,0:T(8,128)(2,1)}), bf16[128,7168]{1,0:T(8,128)(2,1)}) %reduce-scatter.2.cloned.1.call-update) | async-done | bytes 1835024 | tf_op jit(solution)/shard_map/reduce_scatter | solution.py:62
  380.9 2.3 fusion.14
  383.2 0.9 multiply_reduce_fusion
  384.2 2.3 add_convert_fusion
  (34 shorter events, 5.0 us)
Async XLA Ops:
  6.5 10.3 %copy-start.2 = (bf16[128,4096]{1,0:T(8,128)(2,1)S(1)}, bf16[128,4096]{1,0:T(8,128)(2,1)}, u32[]{:S(2)}) copy-start(bf16[128,4096]{1,0:T(8,128)(2,1)} %param.10) | copy-start | bytes 3145732
  6.5 125.5 %all-gather.2.cloned.1.call-start = ((), (), s32[]{:S(2)}) async-start(), calls=%async_computation.4 | async-start | bytes 9175040 | tf_op jit(solution)/shard_map/all_gather | solution.py:61
  9.6 33.0 %all-to-all-start = ((bf16[128,8,512]{2,0,1:T(8,128)(2,1)}), bf16[128,8,512]{2,0,1:T(8,128)(2,1)S(1)}, u32[]{:S(2)}, u32[]{:S(2)}) async-start(bf16[128,8,512]{2,0,1:T(8,128)(2,1)} %bitcast.34), calls=%async_computation | async-start | bytes 2097152 | tf_op jit(solution)/shard_map/all_to_all | solution.py:55
  42.6 29.5 %all-to-all-start.1 = ((bf16[128,8,512]{0,2,1:T(8,128)(2,1)}), bf16[128,8,512]{0,2,1:T(8,128)(2,1)S(1)}, u32[]{:S(2)}, u32[]{:S(2)}) async-start(bf16[128,8,512]{0,2,1:T(8,128)(2,1)} %bitcast.1), calls=%async_computation.1 | async-start | bytes 2097152 | tf_op jit(solution)/shard_map/all_to_all | solution.py:56
  72.1 29.9 %all-to-all-start.2 = ((bf16[128,8,512]{0,2,1:T(8,128)(2,1)}), bf16[128,8,512]{0,2,1:T(8,128)(2,1)}, u32[]{:S(2)}, u32[]{:S(2)}) async-start(bf16[128,8,512]{0,2,1:T(8,128)(2,1)} %bitcast.3), calls=%async_computation.2 | async-start | bytes 2097152 | tf_op jit(solution)/shard_map/all_to_all | solution.py:57
  76.4 304.5 %reduce-scatter.2.cloned.1.call-start = ((), (), s32[]{:S(2)}) async-start(), calls=%async_computation.5 | async-start | bytes 16515072 | tf_op jit(solution)/shard_map/reduce_scatter | solution.py:62
  79.2 26.0 %copy-start.3 = (bf16[1024,4,128]{2,0,1:T(8,128)(2,1)S(1)}, bf16[1024,4,128]{2,0,1:T(8,128)(2,1)}, u32[]{:S(2)}) copy-start(bf16[1024,4,128]{2,0,1:T(8,128)(2,1)} %copy.28) | copy-start | bytes 3145732
  145.3 235.6 %copy-start = (bf16[128,7168]{1,0:T(8,128)(2,1)S(1)}, bf16[128,7168]{1,0:T(8,128)(2,1)}, u32[]{:S(2)}) copy-start(bf16[128,7168]{1,0:T(8,128)(2,1)} %param.12) | copy-start | bytes 5505028
  145.4 238.8 %copy-start.4 = (f32[7168]{0:T(1024)S(1)}, f32[7168]{0:T(1024)}, u32[]{:S(2)}) copy-start(f32[7168]{0:T(1024)} %param.15) | copy-start | bytes 86020
  145.4 238.8 %copy-start.5 = (f32[7168]{0:T(1024)S(1)}, f32[7168]{0:T(1024)}, u32[]{:S(2)}) copy-start(f32[7168]{0:T(1024)} %param.14) | copy-start | bytes 86020
  380.9 2.3 copy-start.1
Sparse Core Ops, SparseCore 0:
  8.9 55.0 all-gather.1
  145.5 235.3 reduce-scatter.1
where the time goes:
time: 394 us; the launch traced here: 393 us
  waiting for transfers between devices  307 us (78%)
  matrix products  34.5 us (9%)
  local copies, waits for them, and re-layouts  15.5 us (4%)
  starting transfers between devices  15.2 us (4%)
  between operations  13.5 us (3%)
  other arithmetic  6.24 us (2%)
    reduce_scatter x1, waiting for transfers between devices, local(): lax.psum_scatter(jnp.dot(attn_heads, group_rows, preferred_element_type=j...  236 us
    all_to_all x1, waiting for transfers between devices, local(): lax.all_to_all(queries, 'ctx', split_axis=1, concat_axis=0, tiled=True)  24.4 us
    all_to_all x1, waiting for transfers between devices, local(): lax.all_to_all(keys, 'ctx', split_axis=1, concat_axis=0, tiled=True)  23.7 us
    all_to_all x1, waiting for transfers between devices, local(): lax.all_to_all(values, 'ctx', split_axis=1, concat_axis=0, tiled=True)  22.8 us
    dot_general x1, matrix products, local(): jnp.dot(attn_heads, group_rows, preferred_element_type=jnp.float32)  13.3 us
    sub x2, matrix products, one_block(): expo = jnp.exp(scores - highest)  10.8 us
    dot_general x2, matrix products, one_block(): jnp.einsum('hqk,khd->qhd', probs, value_heads, preferred_element_type=jnp...  10.4 us
  transfers between devices with their start and end apart: 5, of which 4 were waited for; matrix products, arithmetic and copies ran while one was open for 10% of the time, Pallas kernels for 0%

commit v1 on v0

--- a/solution.py
+++ b/solution.py
@@ -3,6 +3,8 @@
 import jax
 import jax.numpy as jnp
 from jax import lax
+from jax.experimental import pallas as pl
+from jax.experimental.pallas import tpu as pltpu
 from jax.sharding import PartitionSpec as P
 
 HEADS = 32
@@ -50,7 +52,7 @@
     return outputs.reshape(length, width)
 
 
-def local(queries, keys, values, residual_in, out_weight, norm_gain, norm_bias):
+def local_general(queries, keys, values, residual_in, out_weight, norm_gain, norm_bias):
     head_q, head_k, head_v = (
         lax.all_to_all(queries, "ctx", split_axis=1, concat_axis=0, tiled=True),
         lax.all_to_all(keys, "ctx", split_axis=1, concat_axis=0, tiled=True),
@@ -74,6 +76,362 @@
     return normed.astype(jnp.bfloat16)
 
 
+MESH = pl.DeviceIdType.MESH
+CHUNKS = 8
+
+
+def fused_kernel(
+    q_ref, k_ref, v_ref, w_ref, res_ref, gain_ref, bias_ref, out_ref,
+    qh, kh, vh, wf, op, ostage, upr, dnr, ups, dns, own, pbuf,
+    s_send, s_recv, s_local, w_send, w_recv, w_local, o_send, o_recv,
+    up_send, up_recv, dn_send, dn_recv,
+):
+    rows = q_ref.shape[0]
+    hd = qh.shape[2]
+    heads = qh.shape[0]
+    group = heads * hd
+    half = w_ref.shape[0] // 2
+    chunk = own.shape[2]
+    dp = lax.axis_index("dp")
+    ctx = lax.axis_index("ctx")
+    xi, core = dp // 2, dp % 2
+    zi, yi = ctx // 2, ctx % 2
+    sib = (xi * 2 + (1 - core), ctx)
+    xnb = ((1 - xi) * 2 + core, ctx)
+    ynb = (dp, zi * 2 + (1 - yi))
+
+    barrier = pltpu.get_barrier_semaphore()
+    for d in range(1, 8):
+        pl.semaphore_signal(barrier, inc=1, device_id=(dp, (ctx + d) % 8), device_id_type=MESH)
+    for peer in (sib, xnb):
+        pl.semaphore_signal(barrier, inc=1, device_id=peer, device_id_type=MESH)
+    pl.semaphore_wait(barrier, 9)
+
+    sources = (q_ref, k_ref, v_ref)
+    landing = (qh, kh, vh)
+
+    def cols_of(target, h):
+        return pl.ds(pl.multiple_of(target * group + h * hd, hd), hd)
+
+    def rows_of(block):
+        return pl.ds(pl.multiple_of(block * rows, rows), rows)
+
+    def qkv_copy(a, h, target):
+        return pltpu.make_async_remote_copy(
+            src_ref=sources[a].at[:, cols_of(target, h)],
+            dst_ref=landing[a].at[h, rows_of(ctx), :],
+            send_sem=s_send.at[a, h, target],
+            recv_sem=s_recv.at[a, h, ctx],
+            device_id=(dp, target),
+            device_id_type=MESH,
+        )
+
+    def qkv_arrival(a, h, source):
+        place = landing[a].at[h, rows_of(source), :]
+        return pltpu.make_async_remote_copy(
+            src_ref=place, dst_ref=place,
+            send_sem=s_send.at[a, h, source], recv_sem=s_recv.at[a, h, source],
+            device_id=(dp, source), device_id_type=MESH,
+        )
+
+    def qkv_local(a, h):
+        return pltpu.make_async_copy(
+            sources[a].at[:, cols_of(ctx, h)], landing[a].at[h, rows_of(ctx), :], s_local.at[a, h]
+        )
+
+    def w_slot(y, d, part):
+        return wf.at[y, d, pl.ds(part * half, half), :]
+
+    def w_copy(slot_y, slot_d, part, peer, number, first=False):
+        place = w_slot(slot_y, slot_d, part)
+        return pltpu.make_async_remote_copy(
+            src_ref=w_ref.at[pl.ds(part * half, half), :] if first else place,
+            dst_ref=place,
+            send_sem=w_send.at[number, part],
+            recv_sem=w_recv.at[slot_y, slot_d, part],
+            device_id=peer,
+            device_id_type=MESH,
+        )
+
+    def own_w(number, part):
+        return w_copy(yi, dp, part, (xnb, ynb, sib)[number], number, True)
+
+    xdp = xnb[0]
+    forwards = {
+        3: (yi, xdp, sib),
+        4: (1 - yi, dp, sib),
+        5: (1 - yi, dp, xnb),
+        6: (1 - yi, xdp, sib),
+    }
+
+    def forward(number, part):
+        slot_y, slot_d, peer = forwards[number]
+        return w_copy(slot_y, slot_d, part, peer, number)
+
+    keep_w = pltpu.make_async_copy(w_ref, wf.at[yi, dp], w_local.at[0])
+
+    for h in range(heads):
+        for d in (4, 3, 5, 2, 6, 1, 7):
+            for a in range(3):
+                qkv_copy(a, h, (ctx + d) % 8).start()
+        for a in range(3):
+            qkv_local(a, h).start()
+        if h < 3:
+            for part in range(2):
+                own_w(h, part).start()
+    keep_w.start()
+
+    factor = math.log2(math.e) / math.sqrt(hd)
+    block = 2 * rows
+
+    def o_copy(h):
+        return pltpu.make_async_remote_copy(
+            src_ref=ostage.at[h],
+            dst_ref=op.at[yi, h],
+            send_sem=o_send.at[h],
+            recv_sem=o_recv.at[h],
+            device_id=ynb,
+            device_id_type=MESH,
+        )
+
+    def one_head(h, carry):
+        def arrived(d, inner):
+            for a in range(3):
+                qkv_arrival(a, h, (ctx + d) % 8).wait_recv()
+            return inner
+
+        lax.fori_loop(1, 8, arrived, 0)
+        for a in range(3):
+            qkv_local(a, h).wait()
+        for t in range(4):
+            length = block * (t + 1)
+            scores = lax.dot_general(
+                qh[h, t * block : length, :], kh[h, :length, :],
+                (((1,), (1,)), ((), ())), preferred_element_type=jnp.float32,
+            )
+            at_row = lax.broadcasted_iota(jnp.int32, (block, length), 0) + t * block
+            at_col = lax.broadcasted_iota(jnp.int32, (block, length), 1)
+            scores = jnp.where(at_row >= at_col, scores, -1e30)
+            highest = jnp.max(scores, axis=-1, keepdims=True)
+            expo = jnp.exp2((scores - highest) * factor)
+            total = jnp.sum(expo, axis=-1, keepdims=True)
+            result = jnp.dot(
+                expo.astype(jnp.bfloat16), vh[h, :length, :], preferred_element_type=jnp.float32
+            ) / total
+            low, high = result[:rows], result[rows:]
+            mine = jnp.where(yi == 0, low, high)
+            theirs = jnp.where(yi == 0, high, low)
+            op[yi, h, t * rows : (t + 1) * rows, :] = mine.astype(jnp.bfloat16)
+            ostage[h, t * rows : (t + 1) * rows, :] = theirs.astype(jnp.bfloat16)
+        o_copy(h).start()
+
+        @pl.when(h == 1)
+        def _():
+            for part in range(2):
+                w_copy(yi, xdp, part, xnb, 0).wait_recv()
+                forward(3, part).start()
+
+        return carry
+
+    lax.fori_loop(0, heads, one_head, 0)
+
+    for part in range(2):
+        w_copy(1 - yi, dp, part, ynb, 1).wait_recv()
+        forward(5, part).start()
+        forward(4, part).start()
+    for h in range(heads):
+        place = op.at[1 - yi, h]
+        pltpu.make_async_remote_copy(
+            src_ref=place, dst_ref=place, send_sem=o_send.at[h], recv_sem=o_recv.at[h],
+            device_id=ynb, device_id_type=MESH,
+        ).wait_recv()
+    keep_w.wait()
+
+    def chain_copy(up, t, c):
+        slot = t - 1 if up else t
+        to = jnp.minimum(zi + 1, 3) if up else jnp.maximum(zi - 1, 0)
+        return pltpu.make_async_remote_copy(
+            src_ref=(ups if up else dns).at[slot, c],
+            dst_ref=(upr if up else dnr).at[slot, c],
+            send_sem=(up_send if up else dn_send).at[slot, c],
+            recv_sem=(up_recv if up else dn_recv).at[slot, c],
+            device_id=(dp, to * 2 + yi),
+            device_id_type=MESH,
+        )
+
+    def relay(up, t, c, allowed):
+        slot = t - 1 if up else t
+        here, there = (ups, upr) if up else (dns, dnr)
+        sends = jnp.logical_and(allowed, zi < t if up else zi > t)
+        origin = zi == 0 if up else zi == 3
+
+        @pl.when(jnp.logical_and(sends, origin))
+        def _():
+            here[slot, c] = pbuf[t].astype(jnp.bfloat16)
+            chain_copy(up, t, c).start()
+
+        @pl.when(jnp.logical_and(sends, jnp.logical_not(origin)))
+        def _():
+            chain_copy(up, t, c).wait_recv()
+            here[slot, c] = (pbuf[t] + there[slot, c].astype(jnp.float32)).astype(jnp.bfloat16)
+            chain_copy(up, t, c).start()
+
+    def one_chunk(n, carry):
+        i, j = n // 2, n % 2
+        d = ((xi + i // 2) % 2) * 2 + (core + i % 2) % 2
+        c = d * 2 + j
+
+        @pl.when(n % 4 == 2)
+        def _():
+            for y in range(2):
+                for part in range(2):
+                    w_copy(y, d, part, sib, 2).wait_recv()
+
+        @pl.when(n == 3)
+        def _():
+            for part in range(2):
+                w_copy(1 - yi, xdp, part, xnb, 5).wait_recv()
+                forward(6, part).start()
+
+        cols = pl.ds(pl.multiple_of(j * chunk, 128), chunk)
+        lhs = jnp.concatenate([op[y, h] for y in range(2) for h in range(heads)], axis=1)
+        rhs = wf[:, d, :, cols].reshape(2 * group, chunk)
+        pbuf[...] = jnp.dot(lhs, rhs, preferred_element_type=jnp.float32).reshape(pbuf.shape)
+        lower = zi < 2
+        upper = zi >= 2
+        relay(True, 3, c, lower)
+        relay(False, 0, c, upper)
+        relay(True, 3, c, upper)
+        relay(False, 0, c, lower)
+        always = zi >= 0
+        relay(True, 2, c, always)
+        relay(False, 1, c, always)
+        relay(True, 1, c, always)
+        relay(False, 2, c, always)
+        own[c] = pbuf[zi]
+        return carry
+
+    lax.fori_loop(0, CHUNKS, one_chunk, 0)
+
+    width = chunk * CHUNKS
+
+    def arrive(n, carry):
+        i, j = n // 2, n % 2
+        d = ((xi + i // 2) % 2) * 2 + (core + i % 2) % 2
+        c = d * 2 + j
+
+        @pl.when(zi > 0)
+        def _():
+            place = upr.at[zi - 1, c]
+            pltpu.make_async_remote_copy(
+                src_ref=place, dst_ref=place, send_sem=up_send.at[zi - 1, c],
+                recv_sem=up_recv.at[zi - 1, c], device_id=ynb, device_id_type=MESH,
+            ).wait_recv()
+            own[c] += upr[zi - 1, c].astype(jnp.float32)
+
+        @pl.when(zi < 3)
+        def _():
+            place = dnr.at[zi, c]
+            pltpu.make_async_remote_copy(
+                src_ref=place, dst_ref=place, send_sem=dn_send.at[zi, c],
+                recv_sem=dn_recv.at[zi, c], device_id=ynb, device_id_type=MESH,
+            ).wait_recv()
+            own[c] += dnr[zi, c].astype(jnp.float32)
+
+        return carry
+
+    lax.fori_loop(0, CHUNKS, arrive, 0)
+
+    total = jnp.zeros((rows, 1), jnp.float32)
+    for c in range(CHUNKS):
+        res = res_ref[:, c * chunk : (c + 1) * chunk].astype(jnp.float32)
+        mixed = deepnorm_alpha * res + own[c].astype(jnp.bfloat16).astype(jnp.float32)
+        own[c] = mixed
+        total += jnp.sum(mixed, axis=-1, keepdims=True)
+    mean = total / width
+    squares = jnp.zeros((rows, 1), jnp.float32)
+    for c in range(CHUNKS):
+        centered = own[c] - mean
+        squares += jnp.sum(centered * centered, axis=-1, keepdims=True)
+    inverse = lax.rsqrt(squares / width + norm_eps)
+    for c in range(CHUNKS):
+        normed = (own[c] - mean) * inverse * gain_ref[c] + bias_ref[c]
+        out_ref[:, c * chunk : (c + 1) * chunk] = normed.astype(out_ref.dtype)
+
+    def sent_qkv(h, carry):
+        def sent(d, inner):
+            for a in range(3):
+                qkv_copy(a, h, (ctx + d) % 8).wait_send()
+            return inner
+
+        lax.fori_loop(1, 8, sent, 0)
+        o_copy(h).wait_send()
+        return carry
+
+    lax.fori_loop(0, heads, sent_qkv, 0)
+    for part in range(2):
+        for number in range(3):
+            own_w(number, part).wait_send()
+        for number in forwards:
+            forward(number, part).wait_send()
+
+    def sent_chain(c, carry):
+        for t in range(1, 4):
+            @pl.when(zi < t)
+            def _():
+                chain_copy(True, t, c).wait_send()
+        for t in range(3):
+            @pl.when(zi > t)
+            def _():
+                chain_copy(False, t, c).wait_send()
+        return carry
+
+    lax.fori_loop(0, CHUNKS, sent_chain, 0)
+
+
+def local_fused(queries, keys, values, residual_in, out_weight, norm_gain, norm_bias):
+    rows, width = residual_in.shape
+    group, columns = out_weight.shape
+    hd = queries.shape[1] // HEADS
+    heads = group // hd
+    length = rows * 8
+    chunk = width // CHUNKS
+    bf16, f32 = jnp.bfloat16, jnp.float32
+    dma = pltpu.SemaphoreType.DMA
+    in_vmem = pl.BlockSpec(memory_space=pltpu.VMEM)
+    in_any = pl.BlockSpec(memory_space=pl.ANY)
+    return pl.pallas_call(
+        fused_kernel,
+        out_shape=jax.ShapeDtypeStruct((rows, width), bf16),
+        in_specs=[in_any] * 4 + [in_vmem] * 3,
+        out_specs=in_vmem,
+        scratch_shapes=[
+            pltpu.VMEM((heads, length, hd), bf16),
+            pltpu.VMEM((heads, length, hd), bf16),
+            pltpu.VMEM((heads, length, hd), bf16),
+            pltpu.VMEM((2, 4, group, columns), bf16),
+            pltpu.VMEM((2, heads, length // 2, hd), bf16),
+            pltpu.VMEM((heads, length // 2, hd), bf16),
+            pltpu.VMEM((3, CHUNKS, rows, chunk), bf16),
+            pltpu.VMEM((3, CHUNKS, rows, chunk), bf16),
+            pltpu.VMEM((3, CHUNKS, rows, chunk), bf16),
+            pltpu.VMEM((3, CHUNKS, rows, chunk), bf16),
+            pltpu.VMEM((CHUNKS, rows, chunk), f32),
+            pltpu.VMEM((4, rows, chunk), f32),
+            dma((3, heads, 8)), dma((3, heads, 8)), dma((3, heads)),
+            dma((7, 2)), dma((2, 4, 2)), dma((1,)),
+            dma((heads,)), dma((heads,)),
+            dma((3, CHUNKS)), dma((3, CHUNKS)), dma((3, CHUNKS)), dma((3, CHUNKS)),
+        ],
+        compiler_params=pltpu.CompilerParams(
+            collective_id=0, has_side_effects=True, vmem_limit_bytes=60 * 1024 * 1024
+        ),
+    )(
+        queries, keys, values, out_weight, residual_in,
+        norm_gain.reshape(CHUNKS, 1, chunk), norm_bias.reshape(CHUNKS, 1, chunk),
+    )
+
+
 def solution(mesh):
     in_specs = (
         P(("dp", "ctx"), None),
@@ -85,4 +443,6 @@
         P(),
     )
     out_specs = P(("dp", "ctx"), None)
+    fused = mesh.shape["dp"] == 4 and mesh.shape["ctx"] == 8
+    local = local_fused if fused else local_general
     return jax.shard_map(local, mesh=mesh, in_specs=in_specs, out_specs=out_specs, check_vma=False)

time: 394 us -> 226 us (0.57)
  waiting for transfers between devices: 307 us -> 0 us
  Pallas kernels: 0 us -> 223 us
  matrix products: 34.5 us -> 0 us
  starting transfers between devices: 15.2 us -> 0 us
  between operations: 13.5 us -> 0.01 us
  local copies, waits for them, and re-layouts: 15.5 us -> 2.85 us
  other arithmetic: 6.24 us -> 0 us
    reduce_scatter x1 -> x0, waiting for transfers between devices: 236 us -> none  [local(): lax.psum_scatter(jnp.dot(attn_heads, group_rows, preferred_element_type=j...]
    pallas_call x0 -> x1, Pallas kernels: none -> 223 us  [local_fused(): pl.pallas_call(fused_kernel, out_shape=jax.ShapeDtypeStruct((rows, width)...]
    all_to_all x3 -> x0, waiting for transfers between devices: 70.9 us -> none  [the longest x1 24.4 us: local(): lax.all_to_all(queries, 'ctx', split_axis=1, concat_axis=0, tiled=True)]
    dot_general x3 -> x0, matrix products: 23.7 us -> none  [the longest x1 13.3 us: local(): jnp.dot(attn_heads, group_rows, preferred_element_type=jnp.float32)]
    all_to_all x3 -> x0, starting transfers between devices: 15.1 us -> none  [the longest x1 7.28 us: local(): lax.all_to_all(queries, 'ctx', split_axis=1, concat_axis=0, tiled=True)]
    sub x2 -> x0, matrix products: 10.8 us -> none  [one_block(): expo = jnp.exp(scores - highest)]
    all_to_all x3 -> x0, local copies, waits for them, and re-layouts: 4.88 us -> none  [the longest x1 2.29 us: local(): lax.all_to_all(queries, 'ctx', split_axis=1, concat_axis=0, tiled=True)]
  transfers between devices with their start and end apart: 5 -> 0, of which waited for: 4 -> 0; matrix products, arithmetic and copies ran while one was open for 10% -> 0% of each run, Pallas kernels for 0% -> 0%
where the time goes in v1:
time: 226 us
  Pallas kernels  223 us (99%)
  local copies, waits for them, and re-layouts  2.85 us (1%)
    pallas_call x1, Pallas kernels, local_fused(): pl.pallas_call(fused_kernel, out_shape=jax.ShapeDtypeStruct((rows, width)...  223 us

profile of v1, /device:TPU:0, one launch (start us, length us, event | category | flops | bytes accessed | tf_op | source)
XLA Modules:
  0.0 225.8 jit_solution(15251094626108234110)
XLA Ops:
  0.0 223.0 %shard_map.73 = bf16[128,7168]{1,0:T(8,128)(2,1)} custom-call(bf16[128,4096]{1,0:T(8,128)(2,1)} %q_ref.1, bf16[128,4096]{1,0:T(8,128)(2,1)} %k_ref.1, bf16[128,4096]{1,0:T(8,128)(2,1)} %v_ref.1, bf16[512,1792]{1,0:T(8,128)(2,1)} %w_ref.1, bf16[128,7168]{1,0:T(8,128)(2,1)} %res_ref.1, f32[8,1,896]{2,1,0:T(1,128)} %bitcast.2, f32[8,1,896]{2,1,0:T(1,128)} %bitcast.3), custom_call_target="tpu_custom_call" | custom-call | tf_op jit(solution)/shard_map/pallas_call | solution.py:403
  223.0 2.8 %copy.9 = bf16[128,7168]{1,0:T(8,128)(2,1)} copy(bf16[128,7168]{1,0:T(8,128)(2,1)} %shard_map.73) | data formatting | bytes 3670016

commit v2 on v1

--- a/solution.py
+++ b/solution.py
@@ -82,8 +82,9 @@
 
 def fused_kernel(
     q_ref, k_ref, v_ref, w_ref, res_ref, gain_ref, bias_ref, out_ref,
-    qh, kh, vh, wf, op, ostage, upr, dnr, ups, dns, own, pbuf,
-    s_send, s_recv, s_local, w_send, w_recv, w_local, o_send, o_recv,
+    qh, kh, vh, wf, wf2, op, op2, ostage, upr, dnr, stage, own, pbuf,
+    s_send, s_recv, s_local, w_send, w_recv, w_local, w2_send, w2_recv,
+    o_send, o_recv, o2_send, o2_recv,
     up_send, up_recv, dn_send, dn_recv,
 ):
     rows = q_ref.shape[0]
@@ -99,6 +100,10 @@
     sib = (xi * 2 + (1 - core), ctx)
     xnb = ((1 - xi) * 2 + core, ctx)
     ynb = (dp, zi * 2 + (1 - yi))
+    is_hub = jnp.logical_and(zi >= 1, zi <= 2)
+    is_feeder = jnp.logical_or(zi == 0, zi == 3)
+    hub = 1 + zi // 2
+    feeder = (zi // 2) * 3
 
     barrier = pltpu.get_barrier_semaphore()
     for d in range(1, 8):
@@ -139,11 +144,8 @@
             sources[a].at[:, cols_of(ctx, h)], landing[a].at[h, rows_of(ctx), :], s_local.at[a, h]
         )
 
-    def w_slot(y, d, part):
-        return wf.at[y, d, pl.ds(part * half, half), :]
-
     def w_copy(slot_y, slot_d, part, peer, number, first=False):
-        place = w_slot(slot_y, slot_d, part)
+        place = wf.at[slot_y, slot_d, pl.ds(part * half, half), :]
         return pltpu.make_async_remote_copy(
             src_ref=w_ref.at[pl.ds(part * half, half), :] if first else place,
             dst_ref=place,
@@ -167,6 +169,27 @@
     def forward(number, part):
         slot_y, slot_d, peer = forwards[number]
         return w_copy(slot_y, slot_d, part, peer, number)
+
+    def w2_copy(slot_y, slot_d, part, peer, number, first=False):
+        place = wf2.at[slot_y, slot_d, pl.ds(part * half, half), :]
+        return pltpu.make_async_remote_copy(
+            src_ref=w_ref.at[pl.ds(part * half, half), pl.ds(0, chunk)] if first else place,
+            dst_ref=place,
+            send_sem=w2_send.at[number, part],
+            recv_sem=w2_recv.at[slot_y, slot_d, part],
+            device_id=peer,
+            device_id_type=MESH,
+        )
+
+    def feed_w2(part):
+        return w2_copy(yi, dp, part, (dp, hub * 2 + yi), 7, True)
+
+    spreads = {0: (yi, dp, xnb), 1: (yi, dp, ynb), 2: (yi, dp, sib)}
+    spreads.update(forwards)
+
+    def forward2(number, part):
+        slot_y, slot_d, peer = spreads[number]
+        return w2_copy(slot_y, slot_d, part, peer, number)
 
     keep_w = pltpu.make_async_copy(w_ref, wf.at[yi, dp], w_local.at[0])
 
@@ -179,6 +202,11 @@
         if h < 3:
             for part in range(2):
                 own_w(h, part).start()
+        if h == 1:
+            @pl.when(is_feeder)
+            def _():
+                for part in range(2):
+                    feed_w2(part).start()
     keep_w.start()
 
     factor = math.log2(math.e) / math.sqrt(hd)
@@ -191,6 +219,17 @@
             send_sem=o_send.at[h],
             recv_sem=o_recv.at[h],
             device_id=ynb,
+            device_id_type=MESH,
+        )
+
+    def feed_o(h, same):
+        to = yi if same else 1 - yi
+        return pltpu.make_async_remote_copy(
+            src_ref=op.at[yi, h] if same else ostage.at[h],
+            dst_ref=op2.at[yi, h],
+            send_sem=o2_send.at[0 if same else 1, h],
+            recv_sem=o2_recv.at[yi, h],
+            device_id=(dp, hub * 2 + to),
             device_id_type=MESH,
         )
 
@@ -225,6 +264,18 @@
             ostage[h, t * rows : (t + 1) * rows, :] = theirs.astype(jnp.bfloat16)
         o_copy(h).start()
 
+        @pl.when(is_feeder)
+        def _():
+            feed_o(h, True).start()
+            feed_o(h, False).start()
+
+        @pl.when(jnp.logical_and(h == 2, is_hub))
+        def _():
+            for part in range(2):
+                w2_copy(yi, dp, part, ynb, 0).wait_recv()
+                for number in range(3):
+                    forward2(number, part).start()
+
         @pl.when(h == 1)
         def _():
             for part in range(2):
@@ -251,7 +302,7 @@
         slot = t - 1 if up else t
         to = jnp.minimum(zi + 1, 3) if up else jnp.maximum(zi - 1, 0)
         return pltpu.make_async_remote_copy(
-            src_ref=(ups if up else dns).at[slot, c],
+            src_ref=stage.at[slot, c],
             dst_ref=(upr if up else dnr).at[slot, c],
             send_sem=(up_send if up else dn_send).at[slot, c],
             recv_sem=(up_recv if up else dn_recv).at[slot, c],
@@ -259,95 +310,148 @@
             device_id_type=MESH,
         )
 
-    def relay(up, t, c, allowed):
+    def sends_here(up, t, hubs):
+        sends = zi < t if up else zi > t
+        if hubs:
+            sends = jnp.logical_and(sends, zi >= 1 if up else zi <= 2)
+        return sends
+
+    def relay(up, t, c, hubs, allowed):
         slot = t - 1 if up else t
-        here, there = (ups, upr) if up else (dns, dnr)
-        sends = jnp.logical_and(allowed, zi < t if up else zi > t)
-        origin = zi == 0 if up else zi == 3
-
-        @pl.when(jnp.logical_and(sends, origin))
-        def _():
-            here[slot, c] = pbuf[t].astype(jnp.bfloat16)
+        there = upr if up else dnr
+        sends = jnp.logical_and(allowed, sends_here(up, t, hubs))
+        first = (1 if hubs else 0) if up else (2 if hubs else 3)
+
+        @pl.when(jnp.logical_and(sends, zi == first))
+        def _():
+            stage[slot, c] = pbuf[t].astype(jnp.bfloat16)
             chain_copy(up, t, c).start()
 
-        @pl.when(jnp.logical_and(sends, jnp.logical_not(origin)))
+        @pl.when(jnp.logical_and(sends, zi != first))
         def _():
             chain_copy(up, t, c).wait_recv()
-            here[slot, c] = (pbuf[t] + there[slot, c].astype(jnp.float32)).astype(jnp.bfloat16)
+            stage[slot, c] = (pbuf[t] + there[slot, c].astype(jnp.float32)).astype(jnp.bfloat16)
             chain_copy(up, t, c).start()
 
-    def one_chunk(n, carry):
-        i, j = n // 2, n % 2
-        d = ((xi + i // 2) % 2) * 2 + (core + i % 2) % 2
-        c = d * 2 + j
-
-        @pl.when(n % 4 == 2)
+    def relays(c, hubs):
+        lower, upper = zi < 2, zi >= 2
+        ups = (3, 2) if hubs else (3, 2, 1)
+        downs = (0, 1) if hubs else (0, 1, 2)
+        for t in ups:
+            relay(True, t, c, hubs, lower)
+        for t in downs:
+            relay(False, t, c, hubs, upper)
+        for t in ups:
+            relay(True, t, c, hubs, upper)
+        for t in downs:
+            relay(False, t, c, hubs, lower)
+
+    def owner(i):
+        return ((xi + i // 2) % 2) * 2 + (core + i % 2) % 2
+
+    def wait_chain(up, slot, c):
+        place = (upr if up else dnr).at[slot, c]
+        pltpu.make_async_remote_copy(
+            src_ref=place, dst_ref=place, send_sem=(up_send if up else dn_send).at[slot, c],
+            recv_sem=(up_recv if up else dn_recv).at[slot, c], device_id=ynb, device_id_type=MESH,
+        ).wait_recv()
+
+    def finish(i, total):
+        for j in (1, 0):
+            c = owner(i) * 2 + j
+
+            @pl.when(zi > (1 if j == 0 else 0))
+            def _():
+                wait_chain(True, zi - 1, c)
+                own[c] += upr[zi - 1, c].astype(jnp.float32)
+
+            @pl.when(zi < (2 if j == 0 else 3))
+            def _():
+                wait_chain(False, zi, c)
+                own[c] += dnr[zi, c].astype(jnp.float32)
+
+            res = res_ref[:, pl.ds(pl.multiple_of(c * chunk, 128), chunk)].astype(jnp.float32)
+            mixed = deepnorm_alpha * res + own[c].astype(jnp.bfloat16).astype(jnp.float32)
+            own[c] = mixed
+            total = total + jnp.sum(mixed, axis=-1, keepdims=True)
+        return total
+
+    def heads_of(ref):
+        return jnp.concatenate([ref[y, h] for y in range(2) for h in range(heads)], axis=1)
+
+    def product(lhs, rhs):
+        return jnp.dot(
+            lhs, rhs.reshape(2 * group, chunk), preferred_element_type=jnp.float32
+        ).reshape(pbuf.shape)
+
+    def one_step(i, total):
+        d = owner(i)
+
+        @pl.when(i % 2 == 1)
         def _():
             for y in range(2):
                 for part in range(2):
                     w_copy(y, d, part, sib, 2).wait_recv()
 
-        @pl.when(n == 3)
+        c = d * 2 + 1
+        pbuf[...] = product(heads_of(op), wf[:, d, :, pl.ds(chunk, chunk)])
+        relays(c, False)
+        own[c] = pbuf[zi]
+
+        @pl.when(i == 1)
         def _():
             for part in range(2):
                 w_copy(1 - yi, xdp, part, xnb, 5).wait_recv()
                 forward(6, part).start()
 
-        cols = pl.ds(pl.multiple_of(j * chunk, 128), chunk)
-        lhs = jnp.concatenate([op[y, h] for y in range(2) for h in range(heads)], axis=1)
-        rhs = wf[:, d, :, cols].reshape(2 * group, chunk)
-        pbuf[...] = jnp.dot(lhs, rhs, preferred_element_type=jnp.float32).reshape(pbuf.shape)
-        lower = zi < 2
-        upper = zi >= 2
-        relay(True, 3, c, lower)
-        relay(False, 0, c, upper)
-        relay(True, 3, c, upper)
-        relay(False, 0, c, lower)
-        always = zi >= 0
-        relay(True, 2, c, always)
-        relay(False, 1, c, always)
-        relay(True, 1, c, always)
-        relay(False, 2, c, always)
-        own[c] = pbuf[zi]
-        return carry
-
-    lax.fori_loop(0, CHUNKS, one_chunk, 0)
+        c0 = d * 2
+
+        @pl.when(is_hub)
+        def _():
+            @pl.when(i == 0)
+            def _():
+                for part in range(2):
+                    w2_copy(1 - yi, dp, part, ynb, 1).wait_recv()
+                    forward2(5, part).start()
+                    forward2(4, part).start()
+                for part in range(2):
+                    w2_copy(yi, xdp, part, xnb, 0).wait_recv()
+                    forward2(3, part).start()
+                for h in range(heads):
+                    for y in range(2):
+                        place = op2.at[y, h]
+                        pltpu.make_async_remote_copy(
+                            src_ref=place, dst_ref=place, send_sem=o2_send.at[0, h],
+                            recv_sem=o2_recv.at[y, h], device_id=ynb, device_id_type=MESH,
+                        ).wait_recv()
+
+            @pl.when(i % 2 == 1)
+            def _():
+                for y in range(2):
+                    for part in range(2):
+                        w2_copy(y, d, part, sib, 2).wait_recv()
+
+            pbuf[...] = product(heads_of(op), wf[:, d, :, pl.ds(0, chunk)])
+            pbuf[...] += product(heads_of(op2), wf2[:, d])
+            relays(c0, True)
+            own[c0] = pbuf[zi]
+
+            @pl.when(i == 1)
+            def _():
+                for part in range(2):
+                    w2_copy(1 - yi, xdp, part, xnb, 5).wait_recv()
+                    forward2(6, part).start()
+
+        @pl.when(is_feeder)
+        def _():
+            own[c0] = jnp.zeros(own.shape[1:], jnp.float32)
+
+        return lax.cond(i > 0, lambda: finish(i - 1, total), lambda: total)
+
+    total = lax.fori_loop(0, 4, one_step, jnp.zeros((rows, 1), jnp.float32))
+    total = finish(3, total)
 
     width = chunk * CHUNKS
-
-    def arrive(n, carry):
-        i, j = n // 2, n % 2
-        d = ((xi + i // 2) % 2) * 2 + (core + i % 2) % 2
-        c = d * 2 + j
-
-        @pl.when(zi > 0)
-        def _():
-            place = upr.at[zi - 1, c]
-            pltpu.make_async_remote_copy(
-                src_ref=place, dst_ref=place, send_sem=up_send.at[zi - 1, c],
-                recv_sem=up_recv.at[zi - 1, c], device_id=ynb, device_id_type=MESH,
-            ).wait_recv()
-            own[c] += upr[zi - 1, c].astype(jnp.float32)
-
-        @pl.when(zi < 3)
-        def _():
-            place = dnr.at[zi, c]
-            pltpu.make_async_remote_copy(
-                src_ref=place, dst_ref=place, send_sem=dn_send.at[zi, c],
-                recv_sem=dn_recv.at[zi, c], device_id=ynb, device_id_type=MESH,
-            ).wait_recv()
-            own[c] += dnr[zi, c].astype(jnp.float32)
-
-        return carry
-
-    lax.fori_loop(0, CHUNKS, arrive, 0)
-
-    total = jnp.zeros((rows, 1), jnp.float32)
-    for c in range(CHUNKS):
-        res = res_ref[:, c * chunk : (c + 1) * chunk].astype(jnp.float32)
-        mixed = deepnorm_alpha * res + own[c].astype(jnp.bfloat16).astype(jnp.float32)
-        own[c] = mixed
-        total += jnp.sum(mixed, axis=-1, keepdims=True)
     mean = total / width
     squares = jnp.zeros((rows, 1), jnp.float32)
     for c in range(CHUNKS):
@@ -366,6 +470,12 @@
 
         lax.fori_loop(1, 8, sent, 0)
         o_copy(h).wait_send()
+
+        @pl.when(is_feeder)
+        def _():
+            feed_o(h, True).wait_send()
+            feed_o(h, False).wait_send()
+
         return carry
 
     lax.fori_loop(0, heads, sent_qkv, 0)
@@ -375,18 +485,27 @@
         for number in forwards:
             forward(number, part).wait_send()
 
-    def sent_chain(c, carry):
-        for t in range(1, 4):
-            @pl.when(zi < t)
-            def _():
-                chain_copy(True, t, c).wait_send()
-        for t in range(3):
-            @pl.when(zi > t)
-            def _():
-                chain_copy(False, t, c).wait_send()
+    @pl.when(is_feeder)
+    def _():
+        for part in range(2):
+            feed_w2(part).wait_send()
+
+    @pl.when(is_hub)
+    def _():
+        for part in range(2):
+            for number in spreads:
+                forward2(number, part).wait_send()
+
+    def sent_chain(d, carry):
+        for j in range(2):
+            for up, targets in ((True, (3, 2, 1)), (False, (0, 1, 2))):
+                for t in targets:
+                    @pl.when(sends_here(up, t, j == 0))
+                    def _():
+                        chain_copy(up, t, d * 2 + j).wait_send()
         return carry
 
-    lax.fori_loop(0, CHUNKS, sent_chain, 0)
+    lax.fori_loop(0, CHUNKS // 2, sent_chain, 0)
 
 
 def local_fused(queries, keys, values, residual_in, out_weight, norm_gain, norm_bias):
@@ -410,17 +529,18 @@
             pltpu.VMEM((heads, length, hd), bf16),
             pltpu.VMEM((heads, length, hd), bf16),
             pltpu.VMEM((2, 4, group, columns), bf16),
+            pltpu.VMEM((2, 4, group, chunk), bf16),
+            pltpu.VMEM((2, heads, length // 2, hd), bf16),
             pltpu.VMEM((2, heads, length // 2, hd), bf16),
             pltpu.VMEM((heads, length // 2, hd), bf16),
-            pltpu.VMEM((3, CHUNKS, rows, chunk), bf16),
             pltpu.VMEM((3, CHUNKS, rows, chunk), bf16),
             pltpu.VMEM((3, CHUNKS, rows, chunk), bf16),
             pltpu.VMEM((3, CHUNKS, rows, chunk), bf16),
             pltpu.VMEM((CHUNKS, rows, chunk), f32),
             pltpu.VMEM((4, rows, chunk), f32),
             dma((3, heads, 8)), dma((3, heads, 8)), dma((3, heads)),
-            dma((7, 2)), dma((2, 4, 2)), dma((1,)),
-            dma((heads,)), dma((heads,)),
+            dma((7, 2)), dma((2, 4, 2)), dma((1,)), dma((8, 2)), dma((2, 4, 2)),
+            dma((heads,)), dma((heads,)), dma((2, heads)), dma((2, heads)),
             dma((3, CHUNKS)), dma((3, CHUNKS)), dma((3, CHUNKS)), dma((3, CHUNKS)),
         ],
         compiler_params=pltpu.CompilerParams(

time: 226 us -> 216 us (0.956)
  Pallas kernels: 223 us -> 213 us
    pallas_call x1, Pallas kernels: 223 us -> 213 us  [local_fused(): pl.pallas_call(fused_kernel, out_shape=jax.ShapeDtypeStruct((rows, width)...]
where the time goes in v2:
time: 216 us
  Pallas kernels  213 us (99%)
  local copies, waits for them, and re-layouts  2.85 us (1%)
    pallas_call x1, Pallas kernels, local_fused(): pl.pallas_call(fused_kernel, out_shape=jax.ShapeDtypeStruct((rows, width)...  213 us

profile of v2, /device:TPU:0, one launch (start us, length us, event | category | flops | bytes accessed | tf_op | source)
XLA Modules:
  0.0 216.0 jit_solution(6359079850647314046)
XLA Ops:
  0.0 213.1 %shard_map.73 = bf16[128,7168]{1,0:T(8,128)(2,1)} custom-call(bf16[128,4096]{1,0:T(8,128)(2,1)} %q_ref.1, bf16[128,4096]{1,0:T(8,128)(2,1)} %k_ref.1, bf16[128,4096]{1,0:T(8,128)(2,1)} %v_ref.1, bf16[512,1792]{1,0:T(8,128)(2,1)} %w_ref.1, bf16[128,7168]{1,0:T(8,128)(2,1)} %res_ref.1, f32[8,1,896]{2,1,0:T(1,128)} %bitcast.2, f32[8,1,896]{2,1,0:T(1,128)} %bitcast.3), custom_call_target="tpu_custom_call" | custom-call | tf_op jit(solution)/shard_map/pallas_call | solution.py:522
  213.1 2.8 %copy.9 = bf16[128,7168]{1,0:T(8,128)(2,1)} copy(bf16[128,7168]{1,0:T(8,128)(2,1)} %shard_map.73) | data formatting | bytes 3670016

commit v3 on v2

--- a/solution.py
+++ b/solution.py
@@ -82,8 +82,8 @@
 
 def fused_kernel(
     q_ref, k_ref, v_ref, w_ref, res_ref, gain_ref, bias_ref, out_ref,
-    qh, kh, vh, wf, wf2, op, op2, ostage, upr, dnr, stage, own, pbuf,
-    s_send, s_recv, s_local, w_send, w_recv, w_local, w2_send, w2_recv,
+    qh, kh, vh, wf, op, op2, ostage, upr, dnr, stage, own, pbuf,
+    s_send, s_recv, s_local, w_send, w_recv, w_local,
     o_send, o_recv, o2_send, o2_recv,
     up_send, up_recv, dn_send, dn_recv,
 ):
@@ -91,7 +91,6 @@
     hd = qh.shape[2]
     heads = qh.shape[0]
     group = heads * hd
-    half = w_ref.shape[0] // 2
     chunk = own.shape[2]
     dp = lax.axis_index("dp")
     ctx = lax.axis_index("ctx")
@@ -144,22 +143,22 @@
             sources[a].at[:, cols_of(ctx, h)], landing[a].at[h, rows_of(ctx), :], s_local.at[a, h]
         )
 
-    def w_copy(slot_y, slot_d, part, peer, number, first=False):
-        place = wf.at[slot_y, slot_d, pl.ds(part * half, half), :]
+    def w_copy(part, slot_y, slot_d, peer, number, first=False):
+        place = wf.at[part, slot_y, slot_d]
         return pltpu.make_async_remote_copy(
-            src_ref=w_ref.at[pl.ds(part * half, half), :] if first else place,
+            src_ref=w_ref.at[:, pl.ds((part % 2) * chunk, chunk)] if first else place,
             dst_ref=place,
             send_sem=w_send.at[number, part],
-            recv_sem=w_recv.at[slot_y, slot_d, part],
+            recv_sem=w_recv.at[part, slot_y, slot_d],
             device_id=peer,
             device_id_type=MESH,
         )
 
-    def own_w(number, part):
-        return w_copy(yi, dp, part, (xnb, ynb, sib)[number], number, True)
-
     xdp = xnb[0]
-    forwards = {
+    routes = {
+        0: (yi, dp, xnb),
+        1: (yi, dp, ynb),
+        2: (yi, dp, sib),
         3: (yi, xdp, sib),
         4: (1 - yi, dp, sib),
         5: (1 - yi, dp, xnb),
@@ -167,31 +166,19 @@
     }
 
     def forward(number, part):
-        slot_y, slot_d, peer = forwards[number]
-        return w_copy(slot_y, slot_d, part, peer, number)
-
-    def w2_copy(slot_y, slot_d, part, peer, number, first=False):
-        place = wf2.at[slot_y, slot_d, pl.ds(part * half, half), :]
-        return pltpu.make_async_remote_copy(
-            src_ref=w_ref.at[pl.ds(part * half, half), pl.ds(0, chunk)] if first else place,
-            dst_ref=place,
-            send_sem=w2_send.at[number, part],
-            recv_sem=w2_recv.at[slot_y, slot_d, part],
-            device_id=peer,
-            device_id_type=MESH,
-        )
-
-    def feed_w2(part):
-        return w2_copy(yi, dp, part, (dp, hub * 2 + yi), 7, True)
-
-    spreads = {0: (yi, dp, xnb), 1: (yi, dp, ynb), 2: (yi, dp, sib)}
-    spreads.update(forwards)
-
-    def forward2(number, part):
-        slot_y, slot_d, peer = spreads[number]
-        return w2_copy(slot_y, slot_d, part, peer, number)
-
-    keep_w = pltpu.make_async_copy(w_ref, wf.at[yi, dp], w_local.at[0])
+        slot_y, slot_d, peer = routes[number]
+        return w_copy(part, slot_y, slot_d, peer, number, number < 3 and part < 2)
+
+    def w_arrive(part, slot_y, slot_d):
+        w_copy(part, slot_y, slot_d, ynb, 0).wait_recv()
+
+    def feed_w():
+        return w_copy(2, yi, dp, (dp, hub * 2 + yi), 7, True)
+
+    def keep_w(part):
+        return pltpu.make_async_copy(
+            w_ref.at[:, pl.ds(part * chunk, chunk)], wf.at[part, yi, dp], w_local.at[part]
+        )
 
     for h in range(heads):
         for d in (4, 3, 5, 2, 6, 1, 7):
@@ -199,15 +186,21 @@
                 qkv_copy(a, h, (ctx + d) % 8).start()
         for a in range(3):
             qkv_local(a, h).start()
-        if h < 3:
-            for part in range(2):
-                own_w(h, part).start()
+        if h == 0 or h == 2:
+            forward(h, 1).start()
+
+            @pl.when(is_hub)
+            def _():
+                forward(h, 0).start()
+
         if h == 1:
             @pl.when(is_feeder)
             def _():
-                for part in range(2):
-                    feed_w2(part).start()
-    keep_w.start()
+                feed_w().start()
+
+    forward(1, 1).start()
+    for part in range(2):
+        keep_w(part).start()
 
     factor = math.log2(math.e) / math.sqrt(hd)
     block = 2 * rows
@@ -248,9 +241,13 @@
                 qh[h, t * block : length, :], kh[h, :length, :],
                 (((1,), (1,)), ((), ())), preferred_element_type=jnp.float32,
             )
-            at_row = lax.broadcasted_iota(jnp.int32, (block, length), 0) + t * block
-            at_col = lax.broadcasted_iota(jnp.int32, (block, length), 1)
-            scores = jnp.where(at_row >= at_col, scores, -1e30)
+            at_row = lax.broadcasted_iota(jnp.int32, (block, block), 0)
+            at_col = lax.broadcasted_iota(jnp.int32, (block, block), 1)
+            diagonal = jnp.where(at_row >= at_col, scores[:, t * block :], -1e30)
+            if t > 0:
+                scores = jnp.concatenate([scores[:, : t * block], diagonal], axis=1)
+            else:
+                scores = diagonal
             highest = jnp.max(scores, axis=-1, keepdims=True)
             expo = jnp.exp2((scores - highest) * factor)
             total = jnp.sum(expo, axis=-1, keepdims=True)
@@ -269,34 +266,42 @@
             feed_o(h, True).start()
             feed_o(h, False).start()
 
+        @pl.when(h == 1)
+        def _():
+            w_arrive(1, yi, xdp)
+            forward(3, 1).start()
+
+            @pl.when(is_hub)
+            def _():
+                forward(1, 0).start()
+
         @pl.when(jnp.logical_and(h == 2, is_hub))
         def _():
-            for part in range(2):
-                w2_copy(yi, dp, part, ynb, 0).wait_recv()
-                for number in range(3):
-                    forward2(number, part).start()
-
-        @pl.when(h == 1)
-        def _():
-            for part in range(2):
-                w_copy(yi, xdp, part, xnb, 0).wait_recv()
-                forward(3, part).start()
+            w_arrive(0, yi, xdp)
+            forward(3, 0).start()
+            w_arrive(2, yi, dp)
+            forward(0, 2).start()
+            forward(2, 2).start()
 
         return carry
 
     lax.fori_loop(0, heads, one_head, 0)
 
-    for part in range(2):
-        w_copy(1 - yi, dp, part, ynb, 1).wait_recv()
-        forward(5, part).start()
-        forward(4, part).start()
+    @pl.when(is_hub)
+    def _():
+        forward(1, 2).start()
+
+    w_arrive(1, 1 - yi, dp)
+    forward(5, 1).start()
+    forward(4, 1).start()
     for h in range(heads):
         place = op.at[1 - yi, h]
         pltpu.make_async_remote_copy(
             src_ref=place, dst_ref=place, send_sem=o_send.at[h], recv_sem=o_recv.at[h],
             device_id=ynb, device_id_type=MESH,
         ).wait_recv()
-    keep_w.wait()
+    for part in range(2):
+        keep_w(part).wait()
 
     def chain_copy(up, t, c):
         slot = t - 1 if up else t
@@ -347,7 +352,7 @@
             relay(False, t, c, hubs, lower)
 
     def owner(i):
-        return ((xi + i // 2) % 2) * 2 + (core + i % 2) % 2
+        return ((xi + i // 2) % 2) * 2 + (core + i) % 2
 
     def wait_chain(up, slot, c):
         place = (upr if up else dnr).at[slot, c]
@@ -385,70 +390,73 @@
         ).reshape(pbuf.shape)
 
     def one_step(i, total):
-        d = owner(i)
-
-        @pl.when(i % 2 == 1)
-        def _():
-            for y in range(2):
-                for part in range(2):
-                    w_copy(y, d, part, sib, 2).wait_recv()
-
-        c = d * 2 + 1
-        pbuf[...] = product(heads_of(op), wf[:, d, :, pl.ds(chunk, chunk)])
-        relays(c, False)
-        own[c] = pbuf[zi]
-
-        @pl.when(i == 1)
-        def _():
-            for part in range(2):
-                w_copy(1 - yi, xdp, part, xnb, 5).wait_recv()
-                forward(6, part).start()
-
-        c0 = d * 2
-
-        @pl.when(is_hub)
-        def _():
-            @pl.when(i == 0)
-            def _():
-                for part in range(2):
-                    w2_copy(1 - yi, dp, part, ynb, 1).wait_recv()
-                    forward2(5, part).start()
-                    forward2(4, part).start()
-                for part in range(2):
-                    w2_copy(yi, xdp, part, xnb, 0).wait_recv()
-                    forward2(3, part).start()
-                for h in range(heads):
-                    for y in range(2):
-                        place = op2.at[y, h]
-                        pltpu.make_async_remote_copy(
-                            src_ref=place, dst_ref=place, send_sem=o2_send.at[0, h],
-                            recv_sem=o2_recv.at[y, h], device_id=ynb, device_id_type=MESH,
-                        ).wait_recv()
+        @pl.when(i < 4)
+        def _():
+            d = owner(i)
 
             @pl.when(i % 2 == 1)
             def _():
                 for y in range(2):
-                    for part in range(2):
-                        w2_copy(y, d, part, sib, 2).wait_recv()
-
-            pbuf[...] = product(heads_of(op), wf[:, d, :, pl.ds(0, chunk)])
-            pbuf[...] += product(heads_of(op2), wf2[:, d])
-            relays(c0, True)
-            own[c0] = pbuf[zi]
+                    w_arrive(1, y, d)
+
+            pbuf[...] = product(heads_of(op), wf[1, :, d])
+            relays(d * 2 + 1, False)
+            own[d * 2 + 1] = pbuf[zi]
 
             @pl.when(i == 1)
             def _():
-                for part in range(2):
-                    w2_copy(1 - yi, xdp, part, xnb, 5).wait_recv()
-                    forward2(6, part).start()
-
-        @pl.when(is_feeder)
-        def _():
-            own[c0] = jnp.zeros(own.shape[1:], jnp.float32)
-
-        return lax.cond(i > 0, lambda: finish(i - 1, total), lambda: total)
-
-    total = lax.fori_loop(0, 4, one_step, jnp.zeros((rows, 1), jnp.float32))
+                w_arrive(1, 1 - yi, xdp)
+                forward(6, 1).start()
+
+        @pl.when(jnp.logical_and(i == 0, is_hub))
+        def _():
+            w_arrive(0, 1 - yi, dp)
+            forward(5, 0).start()
+            forward(4, 0).start()
+            w_arrive(2, yi, xdp)
+            forward(3, 2).start()
+
+        @pl.when(jnp.logical_and(i == 1, is_hub))
+        def _():
+            w_arrive(2, 1 - yi, dp)
+            forward(5, 2).start()
+            forward(4, 2).start()
+            for h in range(heads):
+                for y in range(2):
+                    place = op2.at[y, h]
+                    pltpu.make_async_remote_copy(
+                        src_ref=place, dst_ref=place, send_sem=o2_send.at[0, h],
+                        recv_sem=o2_recv.at[y, h], device_id=ynb, device_id_type=MESH,
+                    ).wait_recv()
+
+        @pl.when(jnp.logical_and(i >= 1, is_hub))
+        def _():
+            d = owner(i - 1)
+
+            @pl.when(i % 2 == 0)
+            def _():
+                for y in range(2):
+                    w_arrive(0, y, d)
+                    w_arrive(2, y, d)
+
+            pbuf[...] = product(heads_of(op), wf[0, :, d])
+            pbuf[...] += product(heads_of(op2), wf[2, :, d])
+            relays(d * 2, True)
+            own[d * 2] = pbuf[zi]
+
+            @pl.when(i == 2)
+            def _():
+                for part in (0, 2):
+                    w_arrive(part, 1 - yi, xdp)
+                    forward(6, part).start()
+
+        @pl.when(jnp.logical_and(i >= 1, is_feeder))
+        def _():
+            own[owner(i - 1) * 2] = jnp.zeros(own.shape[1:], jnp.float32)
+
+        return lax.cond(i > 1, lambda: finish(i - 2, total), lambda: total)
+
+    total = lax.fori_loop(0, 5, one_step, jnp.zeros((rows, 1), jnp.float32))
     total = finish(3, total)
 
     width = chunk * CHUNKS
@@ -479,22 +487,18 @@
         return carry
 
     lax.fori_loop(0, heads, sent_qkv, 0)
-    for part in range(2):
-        for number in range(3):
-            own_w(number, part).wait_send()
-        for number in forwards:
-            forward(number, part).wait_send()
+    for number in routes:
+        forward(number, 1).wait_send()
 
     @pl.when(is_feeder)
     def _():
-        for part in range(2):
-            feed_w2(part).wait_send()
+        feed_w().wait_send()
 
     @pl.when(is_hub)
     def _():
-        for part in range(2):
-            for number in spreads:
-                forward2(number, part).wait_send()
+        for number in routes:
+            for part in (0, 2):
+                forward(number, part).wait_send()
 
     def sent_chain(d, carry):
         for j in range(2):
@@ -528,8 +532,7 @@
             pltpu.VMEM((heads, length, hd), bf16),
             pltpu.VMEM((heads, length, hd), bf16),
             pltpu.VMEM((heads, length, hd), bf16),
-            pltpu.VMEM((2, 4, group, columns), bf16),
-            pltpu.VMEM((2, 4, group, chunk), bf16),
+            pltpu.VMEM((3, 2, 4, group, chunk), bf16),
             pltpu.VMEM((2, heads, length // 2, hd), bf16),
             pltpu.VMEM((2, heads, length // 2, hd), bf16),
             pltpu.VMEM((heads, length // 2, hd), bf16),
@@ -539,7 +542,7 @@
             pltpu.VMEM((CHUNKS, rows, chunk), f32),
             pltpu.VMEM((4, rows, chunk), f32),
             dma((3, heads, 8)), dma((3, heads, 8)), dma((3, heads)),
-            dma((7, 2)), dma((2, 4, 2)), dma((1,)), dma((8, 2)), dma((2, 4, 2)),
+            dma((8, 3)), dma((3, 2, 4)), dma((2,)),
             dma((heads,)), dma((heads,)), dma((2, heads)), dma((2, heads)),
             dma((3, CHUNKS)), dma((3, CHUNKS)), dma((3, CHUNKS)), dma((3, CHUNKS)),
         ],

time: 216 us -> 203 us (0.940)
  Pallas kernels: 213 us -> 200 us
    pallas_call x1, Pallas kernels: 213 us -> 200 us  [local_fused(): pl.pallas_call(fused_kernel, out_shape=jax.ShapeDtypeStruct((rows, width)...]
where the time goes in v3:
time: 203 us; the launch traced here: 202 us
  Pallas kernels  200 us (99%)
  local copies, waits for them, and re-layouts  2.85 us (1%)
    pallas_call x1, Pallas kernels, local_fused(): pl.pallas_call(fused_kernel, out_shape=jax.ShapeDtypeStruct((rows, width)...  200 us

profile of v3, /device:TPU:0, one launch (start us, length us, event | category | flops | bytes accessed | tf_op | source)
XLA Modules:
  0.0 202.4 jit_solution(15365595241582462475)
XLA Ops:
  0.0 199.6 %shard_map.73 = bf16[128,7168]{1,0:T(8,128)(2,1)} custom-call(bf16[128,4096]{1,0:T(8,128)(2,1)} %q_ref.1, bf16[128,4096]{1,0:T(8,128)(2,1)} %k_ref.1, bf16[128,4096]{1,0:T(8,128)(2,1)} %v_ref.1, bf16[512,1792]{1,0:T(8,128)(2,1)} %w_ref.1, bf16[128,7168]{1,0:T(8,128)(2,1)} %res_ref.1, f32[8,1,896]{2,1,0:T(1,128)} %bitcast.2, f32[8,1,896]{2,1,0:T(1,128)} %bitcast.3), custom_call_target="tpu_custom_call" | custom-call | tf_op jit(solution)/shard_map/pallas_call | solution.py:526
  199.6 2.8 %copy.9 = bf16[128,7168]{1,0:T(8,128)(2,1)} copy(bf16[128,7168]{1,0:T(8,128)(2,1)} %shard_map.73) | data formatting | bytes 3670016

commit v4 on v3

--- a/solution.py
+++ b/solution.py
@@ -77,12 +77,13 @@
 
 
 MESH = pl.DeviceIdType.MESH
-CHUNKS = 8
 
 
 def fused_kernel(
     q_ref, k_ref, v_ref, w_ref, res_ref, gain_ref, bias_ref, out_ref,
-    qh, kh, vh, wf, op, op2, ostage, upr, dnr, stage, own, pbuf,
+    qh, kh, vh, wf_hub, wf_chain, op, op2, ostage,
+    upr_hub, dnr_hub, stage_hub, own_hub, pbuf_hub,
+    upr_chain, dnr_chain, stage_chain, own_chain, pbuf_chain,
     s_send, s_recv, s_local, w_send, w_recv, w_local,
     o_send, o_recv, o2_send, o2_recv,
     up_send, up_recv, dn_send, dn_recv,
@@ -91,7 +92,12 @@
     hd = qh.shape[2]
     heads = qh.shape[0]
     group = heads * hd
-    chunk = own.shape[2]
+    columns = w_ref.shape[1]
+    chunks = (own_hub.shape[2], own_chain.shape[2])
+    starts = (0, chunks[0])
+    uprs, dnrs = (upr_hub, upr_chain), (dnr_hub, dnr_chain)
+    stages, owns = (stage_hub, stage_chain), (own_hub, own_chain)
+    pbufs = (pbuf_hub, pbuf_chain)
     dp = lax.axis_index("dp")
     ctx = lax.axis_index("ctx")
     xi, core = dp // 2, dp % 2
@@ -143,10 +149,13 @@
             sources[a].at[:, cols_of(ctx, h)], landing[a].at[h, rows_of(ctx), :], s_local.at[a, h]
         )
 
+    def w_place(part, slot_y, slot_d):
+        return wf_chain.at[slot_y, slot_d] if part == 1 else wf_hub.at[part // 2, slot_y, slot_d]
+
     def w_copy(part, slot_y, slot_d, peer, number, first=False):
-        place = wf.at[part, slot_y, slot_d]
+        place = w_place(part, slot_y, slot_d)
         return pltpu.make_async_remote_copy(
-            src_ref=w_ref.at[:, pl.ds((part % 2) * chunk, chunk)] if first else place,
+            src_ref=w_ref.at[:, pl.ds(starts[part % 2], chunks[part % 2])] if first else place,
             dst_ref=place,
             send_sem=w_send.at[number, part],
             recv_sem=w_recv.at[part, slot_y, slot_d],
@@ -177,7 +186,7 @@
 
     def keep_w(part):
         return pltpu.make_async_copy(
-            w_ref.at[:, pl.ds(part * chunk, chunk)], wf.at[part, yi, dp], w_local.at[part]
+            w_ref.at[:, pl.ds(starts[part], chunks[part])], w_place(part, yi, dp), w_local.at[part]
         )
 
     for h in range(heads):
@@ -194,11 +203,12 @@
                 forward(h, 0).start()
 
         if h == 1:
+            forward(1, 1).start()
+
             @pl.when(is_feeder)
             def _():
                 feed_w().start()
 
-    forward(1, 1).start()
     for part in range(2):
         keep_w(part).start()
 
@@ -215,16 +225,26 @@
             device_id_type=MESH,
         )
 
-    def feed_o(h, same):
-        to = yi if same else 1 - yi
+    def feed_o(h, y):
         return pltpu.make_async_remote_copy(
-            src_ref=op.at[yi, h] if same else ostage.at[h],
-            dst_ref=op2.at[yi, h],
-            send_sem=o2_send.at[0 if same else 1, h],
-            recv_sem=o2_recv.at[yi, h],
-            device_id=(dp, hub * 2 + to),
+            src_ref=op.at[y, h],
+            dst_ref=op2.at[y, h],
+            send_sem=o2_send.at[y, h],
+            recv_sem=o2_recv.at[y, h],
+            device_id=(dp, hub * 2 + yi),
             device_id_type=MESH,
         )
+
+    def other_half(h):
+        place = op.at[1 - yi, h]
+        pltpu.make_async_remote_copy(
+            src_ref=place, dst_ref=place, send_sem=o_send.at[h], recv_sem=o_recv.at[h],
+            device_id=ynb, device_id_type=MESH,
+        ).wait_recv()
+
+        @pl.when(is_feeder)
+        def _():
+            feed_o(h, 1 - yi).start()
 
     def one_head(h, carry):
         def arrived(d, inner):
@@ -263,8 +283,11 @@
 
         @pl.when(is_feeder)
         def _():
-            feed_o(h, True).start()
-            feed_o(h, False).start()
+            feed_o(h, yi).start()
+
+        @pl.when(h > 0)
+        def _():
+            other_half(h - 1)
 
         @pl.when(h == 1)
         def _():
@@ -294,23 +317,18 @@
     w_arrive(1, 1 - yi, dp)
     forward(5, 1).start()
     forward(4, 1).start()
-    for h in range(heads):
-        place = op.at[1 - yi, h]
-        pltpu.make_async_remote_copy(
-            src_ref=place, dst_ref=place, send_sem=o_send.at[h], recv_sem=o_recv.at[h],
-            device_id=ynb, device_id_type=MESH,
-        ).wait_recv()
+    other_half(heads - 1)
     for part in range(2):
         keep_w(part).wait()
 
-    def chain_copy(up, t, c):
+    def chain_copy(up, t, j, d):
         slot = t - 1 if up else t
         to = jnp.minimum(zi + 1, 3) if up else jnp.maximum(zi - 1, 0)
         return pltpu.make_async_remote_copy(
-            src_ref=stage.at[slot, c],
-            dst_ref=(upr if up else dnr).at[slot, c],
-            send_sem=(up_send if up else dn_send).at[slot, c],
-            recv_sem=(up_recv if up else dn_recv).at[slot, c],
+            src_ref=stages[j].at[slot, d],
+            dst_ref=(uprs if up else dnrs)[j].at[slot, d],
+            send_sem=(up_send if up else dn_send).at[slot, d * 2 + j],
+            recv_sem=(up_recv if up else dn_recv).at[slot, d * 2 + j],
             device_id=(dp, to * 2 + yi),
             device_id_type=MESH,
         )
@@ -321,63 +339,68 @@
             sends = jnp.logical_and(sends, zi >= 1 if up else zi <= 2)
         return sends
 
-    def relay(up, t, c, hubs, allowed):
+    def relay(up, t, j, d, allowed):
+        hubs = j == 0
         slot = t - 1 if up else t
-        there = upr if up else dnr
+        there, stage, pbuf = (uprs if up else dnrs)[j], stages[j], pbufs[j]
         sends = jnp.logical_and(allowed, sends_here(up, t, hubs))
         first = (1 if hubs else 0) if up else (2 if hubs else 3)
 
         @pl.when(jnp.logical_and(sends, zi == first))
         def _():
-            stage[slot, c] = pbuf[t].astype(jnp.bfloat16)
-            chain_copy(up, t, c).start()
+            stage[slot, d] = pbuf[t].astype(jnp.bfloat16)
+            chain_copy(up, t, j, d).start()
 
         @pl.when(jnp.logical_and(sends, zi != first))
         def _():
-            chain_copy(up, t, c).wait_recv()
-            stage[slot, c] = (pbuf[t] + there[slot, c].astype(jnp.float32)).astype(jnp.bfloat16)
-            chain_copy(up, t, c).start()
-
-    def relays(c, hubs):
+            chain_copy(up, t, j, d).wait_recv()
+            stage[slot, d] = (pbuf[t] + there[slot, d].astype(jnp.float32)).astype(jnp.bfloat16)
+            chain_copy(up, t, j, d).start()
+
+    def relays(j, d):
+        hubs = j == 0
         lower, upper = zi < 2, zi >= 2
         ups = (3, 2) if hubs else (3, 2, 1)
         downs = (0, 1) if hubs else (0, 1, 2)
         for t in ups:
-            relay(True, t, c, hubs, lower)
+            relay(True, t, j, d, lower)
         for t in downs:
-            relay(False, t, c, hubs, upper)
+            relay(False, t, j, d, upper)
         for t in ups:
-            relay(True, t, c, hubs, upper)
+            relay(True, t, j, d, upper)
         for t in downs:
-            relay(False, t, c, hubs, lower)
+            relay(False, t, j, d, lower)
 
     def owner(i):
         return ((xi + i // 2) % 2) * 2 + (core + i) % 2
 
-    def wait_chain(up, slot, c):
-        place = (upr if up else dnr).at[slot, c]
+    def wait_chain(up, slot, j, d):
+        place = (uprs if up else dnrs)[j].at[slot, d]
+        at = d * 2 + j
         pltpu.make_async_remote_copy(
-            src_ref=place, dst_ref=place, send_sem=(up_send if up else dn_send).at[slot, c],
-            recv_sem=(up_recv if up else dn_recv).at[slot, c], device_id=ynb, device_id_type=MESH,
+            src_ref=place, dst_ref=place, send_sem=(up_send if up else dn_send).at[slot, at],
+            recv_sem=(up_recv if up else dn_recv).at[slot, at], device_id=ynb, device_id_type=MESH,
         ).wait_recv()
 
     def finish(i, total):
+        d = owner(i)
         for j in (1, 0):
-            c = owner(i) * 2 + j
+            own = owns[j]
 
             @pl.when(zi > (1 if j == 0 else 0))
             def _():
-                wait_chain(True, zi - 1, c)
-                own[c] += upr[zi - 1, c].astype(jnp.float32)
+                wait_chain(True, zi - 1, j, d)
+                own[d] += uprs[j][zi - 1, d].astype(jnp.float32)
 
             @pl.when(zi < (2 if j == 0 else 3))
             def _():
-                wait_chain(False, zi, c)
-                own[c] += dnr[zi, c].astype(jnp.float32)
-
-            res = res_ref[:, pl.ds(pl.multiple_of(c * chunk, 128), chunk)].astype(jnp.float32)
-            mixed = deepnorm_alpha * res + own[c].astype(jnp.bfloat16).astype(jnp.float32)
-            own[c] = mixed
+                wait_chain(False, zi, j, d)
+                own[d] += dnrs[j][zi, d].astype(jnp.float32)
+
+            cols = pl.ds(pl.multiple_of(d * columns + starts[j], 128), chunks[j])
+            res = res_ref[:, cols].astype(jnp.float32)
+            mixed = deepnorm_alpha * res + own[d].astype(jnp.bfloat16).astype(jnp.float32)
+            own[d] = mixed
             total = total + jnp.sum(mixed, axis=-1, keepdims=True)
         return total
 
@@ -385,28 +408,27 @@
         return jnp.concatenate([ref[y, h] for y in range(2) for h in range(heads)], axis=1)
 
     def product(lhs, rhs):
+        wide = rhs.shape[-1]
         return jnp.dot(
-            lhs, rhs.reshape(2 * group, chunk), preferred_element_type=jnp.float32
-        ).reshape(pbuf.shape)
+            lhs, rhs.reshape(2 * group, wide), preferred_element_type=jnp.float32
+        ).reshape(4, rows, wide)
 
     def one_step(i, total):
-        @pl.when(i < 4)
-        def _():
-            d = owner(i)
-
-            @pl.when(i % 2 == 1)
-            def _():
-                for y in range(2):
-                    w_arrive(1, y, d)
-
-            pbuf[...] = product(heads_of(op), wf[1, :, d])
-            relays(d * 2 + 1, False)
-            own[d * 2 + 1] = pbuf[zi]
-
-            @pl.when(i == 1)
-            def _():
-                w_arrive(1, 1 - yi, xdp)
-                forward(6, 1).start()
+        d = owner(i)
+
+        @pl.when(i % 2 == 1)
+        def _():
+            for y in range(2):
+                w_arrive(1, y, d)
+
+        pbuf_chain[...] = product(heads_of(op), wf_chain[:, d])
+        relays(1, d)
+        own_chain[d] = pbuf_chain[zi]
+
+        @pl.when(i == 1)
+        def _():
+            w_arrive(1, 1 - yi, xdp)
+            forward(6, 1).start()
 
         @pl.when(jnp.logical_and(i == 0, is_hub))
         def _():
@@ -415,9 +437,6 @@
             forward(4, 0).start()
             w_arrive(2, yi, xdp)
             forward(3, 2).start()
-
-        @pl.when(jnp.logical_and(i == 1, is_hub))
-        def _():
             w_arrive(2, 1 - yi, dp)
             forward(5, 2).start()
             forward(4, 2).start()
@@ -429,46 +448,48 @@
                         recv_sem=o2_recv.at[y, h], device_id=ynb, device_id_type=MESH,
                     ).wait_recv()
 
-        @pl.when(jnp.logical_and(i >= 1, is_hub))
-        def _():
-            d = owner(i - 1)
-
-            @pl.when(i % 2 == 0)
+        @pl.when(is_hub)
+        def _():
+            @pl.when(i % 2 == 1)
             def _():
                 for y in range(2):
                     w_arrive(0, y, d)
                     w_arrive(2, y, d)
 
-            pbuf[...] = product(heads_of(op), wf[0, :, d])
-            pbuf[...] += product(heads_of(op2), wf[2, :, d])
-            relays(d * 2, True)
-            own[d * 2] = pbuf[zi]
-
-            @pl.when(i == 2)
+            pbuf_hub[...] = product(heads_of(op), wf_hub[0, :, d])
+            pbuf_hub[...] += product(heads_of(op2), wf_hub[1, :, d])
+            relays(0, d)
+            own_hub[d] = pbuf_hub[zi]
+
+            @pl.when(i == 1)
             def _():
                 for part in (0, 2):
                     w_arrive(part, 1 - yi, xdp)
                     forward(6, part).start()
 
-        @pl.when(jnp.logical_and(i >= 1, is_feeder))
-        def _():
-            own[owner(i - 1) * 2] = jnp.zeros(own.shape[1:], jnp.float32)
-
-        return lax.cond(i > 1, lambda: finish(i - 2, total), lambda: total)
-
-    total = lax.fori_loop(0, 5, one_step, jnp.zeros((rows, 1), jnp.float32))
+        @pl.when(is_feeder)
+        def _():
+            own_hub[d] = jnp.zeros(own_hub.shape[1:], jnp.float32)
+
+        return lax.cond(i > 0, lambda: finish(i - 1, total), lambda: total)
+
+    total = lax.fori_loop(0, 4, one_step, jnp.zeros((rows, 1), jnp.float32))
     total = finish(3, total)
 
-    width = chunk * CHUNKS
+    width = columns * 4
     mean = total / width
     squares = jnp.zeros((rows, 1), jnp.float32)
-    for c in range(CHUNKS):
-        centered = own[c] - mean
-        squares += jnp.sum(centered * centered, axis=-1, keepdims=True)
+    for own in owns:
+        for d in range(4):
+            centered = own[d] - mean
+            squares += jnp.sum(centered * centered, axis=-1, keepdims=True)
     inverse = lax.rsqrt(squares / width + norm_eps)
-    for c in range(CHUNKS):
-        normed = (own[c] - mean) * inverse * gain_ref[c] + bias_ref[c]
-        out_ref[:, c * chunk : (c + 1) * chunk] = normed.astype(out_ref.dtype)
+    for j, own in enumerate(owns):
+        for d in range(4):
+            low = d * columns + starts[j]
+            cols = slice(low, low + chunks[j])
+            normed = (own[d] - mean) * inverse * gain_ref[:, cols] + bias_ref[:, cols]
+            out_ref[:, cols] = normed.astype(out_ref.dtype)
 
     def sent_qkv(h, carry):
         def sent(d, inner):
@@ -481,8 +502,8 @@
 
         @pl.when(is_feeder)
         def _():
-            feed_o(h, True).wait_send()
-            feed_o(h, False).wait_send()
+            feed_o(h, 0).wait_send()
+            feed_o(h, 1).wait_send()
 
         return carry
 
@@ -506,10 +527,10 @@
                 for t in targets:
                     @pl.when(sends_here(up, t, j == 0))
                     def _():
-                        chain_copy(up, t, d * 2 + j).wait_send()
+                        chain_copy(up, t, j, d).wait_send()
         return carry
 
-    lax.fori_loop(0, CHUNKS // 2, sent_chain, 0)
+    lax.fori_loop(0, 4, sent_chain, 0)
 
 
 def local_fused(queries, keys, values, residual_in, out_weight, norm_gain, norm_bias):
@@ -518,7 +539,8 @@
     hd = queries.shape[1] // HEADS
     heads = group // hd
     length = rows * 8
-    chunk = width // CHUNKS
+    hub_part = columns // 7 * 4
+    chain_part = columns - hub_part
     bf16, f32 = jnp.bfloat16, jnp.float32
     dma = pltpu.SemaphoreType.DMA
     in_vmem = pl.BlockSpec(memory_space=pltpu.VMEM)
@@ -532,26 +554,27 @@
             pltpu.VMEM((heads, length, hd), bf16),
             pltpu.VMEM((heads, length, hd), bf16),
             pltpu.VMEM((heads, length, hd), bf16),
-            pltpu.VMEM((3, 2, 4, group, chunk), bf16),
+            pltpu.VMEM((2, 2, 4, group, hub_part), bf16),
+            pltpu.VMEM((2, 4, group, chain_part), bf16),
             pltpu.VMEM((2, heads, length // 2, hd), bf16),
             pltpu.VMEM((2, heads, length // 2, hd), bf16),
             pltpu.VMEM((heads, length // 2, hd), bf16),
-            pltpu.VMEM((3, CHUNKS, rows, chunk), bf16),
-            pltpu.VMEM((3, CHUNKS, rows, chunk), bf16),
-            pltpu.VMEM((3, CHUNKS, rows, chunk), bf16),
-            pltpu.VMEM((CHUNKS, rows, chunk), f32),
-            pltpu.VMEM((4, rows, chunk), f32),
+        ] + [
+            pltpu.VMEM(shape + (rows, part), kind)
+            for part in (hub_part, chain_part)
+            for shape, kind in (((3, 4), bf16),) * 3 + (((4,), f32),) * 2
+        ] + [
             dma((3, heads, 8)), dma((3, heads, 8)), dma((3, heads)),
             dma((8, 3)), dma((3, 2, 4)), dma((2,)),
             dma((heads,)), dma((heads,)), dma((2, heads)), dma((2, heads)),
-            dma((3, CHUNKS)), dma((3, CHUNKS)), dma((3, CHUNKS)), dma((3, CHUNKS)),
+            dma((3, 8)), dma((3, 8)), dma((3, 8)), dma((3, 8)),
         ],
         compiler_params=pltpu.CompilerParams(
             collective_id=0, has_side_effects=True, vmem_limit_bytes=60 * 1024 * 1024
         ),
     )(
         queries, keys, values, out_weight, residual_in,
-        norm_gain.reshape(CHUNKS, 1, chunk), norm_bias.reshape(CHUNKS, 1, chunk),
+        norm_gain.reshape(1, width), norm_bias.reshape(1, width),
     )
 
 

time: 203 us -> 211 us (1.039)
  Pallas kernels: 200 us -> 208 us
    pallas_call x1, Pallas kernels: 200 us -> 208 us  [local_fused(): pl.pallas_call(fused_kernel, out_shape=jax.ShapeDtypeStruct((rows, width)...]
where the time goes in v4:
time: 211 us
  Pallas kernels  208 us (99%)
  local copies, waits for them, and re-layouts  2.85 us (1%)
    pallas_call x1, Pallas kernels, local_fused(): pl.pallas_call(fused_kernel, out_shape=jax.ShapeDtypeStruct((rows, width)...  208 us

profile of v4, /device:TPU:0, one launch (start us, length us, event | category | flops | bytes accessed | tf_op | source)
XLA Modules:
  0.0 210.7 jit_solution(10674163495790630405)
XLA Ops:
  0.0 207.9 %shard_map.73 = bf16[128,7168]{1,0:T(8,128)(2,1)} custom-call(bf16[128,4096]{1,0:T(8,128)(2,1)} %q_ref.1, bf16[128,4096]{1,0:T(8,128)(2,1)} %k_ref.1, bf16[128,4096]{1,0:T(8,128)(2,1)} %v_ref.1, bf16[512,1792]{1,0:T(8,128)(2,1)} %w_ref.1, bf16[128,7168]{1,0:T(8,128)(2,1)} %res_ref.1, f32[1,7168]{1,0:T(1,128)} %bitcast.2, f32[1,7168]{1,0:T(1,128)} %bitcast.3), custom_call_target="tpu_custom_call" | custom-call | tf_op jit(solution)/shard_map/pallas_call | solution.py:548
  207.9 2.8 %copy.9 = bf16[128,7168]{1,0:T(8,128)(2,1)} copy(bf16[128,7168]{1,0:T(8,128)(2,1)} %shard_map.73) | data formatting | bytes 3670016

commit v5 on v4

--- a/solution.py
+++ b/solution.py
@@ -414,21 +414,23 @@
         ).reshape(4, rows, wide)
 
     def one_step(i, total):
-        d = owner(i)
-
-        @pl.when(i % 2 == 1)
-        def _():
-            for y in range(2):
-                w_arrive(1, y, d)
-
-        pbuf_chain[...] = product(heads_of(op), wf_chain[:, d])
-        relays(1, d)
-        own_chain[d] = pbuf_chain[zi]
-
-        @pl.when(i == 1)
-        def _():
-            w_arrive(1, 1 - yi, xdp)
-            forward(6, 1).start()
+        @pl.when(i < 4)
+        def _():
+            d = owner(i)
+
+            @pl.when(i % 2 == 1)
+            def _():
+                for y in range(2):
+                    w_arrive(1, y, d)
+
+            pbuf_chain[...] = product(heads_of(op), wf_chain[:, d])
+            relays(1, d)
+            own_chain[d] = pbuf_chain[zi]
+
+            @pl.when(i == 1)
+            def _():
+                w_arrive(1, 1 - yi, xdp)
+                forward(6, 1).start()
 
         @pl.when(jnp.logical_and(i == 0, is_hub))
         def _():
@@ -437,6 +439,9 @@
             forward(4, 0).start()
             w_arrive(2, yi, xdp)
             forward(3, 2).start()
+
+        @pl.when(jnp.logical_and(i == 1, is_hub))
+        def _():
             w_arrive(2, 1 - yi, dp)
             forward(5, 2).start()
             forward(4, 2).start()
@@ -448,9 +453,11 @@
                         recv_sem=o2_recv.at[y, h], device_id=ynb, device_id_type=MESH,
                     ).wait_recv()
 
-        @pl.when(is_hub)
-        def _():
-            @pl.when(i % 2 == 1)
+        @pl.when(jnp.logical_and(i >= 1, is_hub))
+        def _():
+            d = owner(i - 1)
+
+            @pl.when(i % 2 == 0)
             def _():
                 for y in range(2):
                     w_arrive(0, y, d)
@@ -461,19 +468,19 @@
             relays(0, d)
             own_hub[d] = pbuf_hub[zi]
 
-            @pl.when(i == 1)
+            @pl.when(i == 2)
             def _():
                 for part in (0, 2):
                     w_arrive(part, 1 - yi, xdp)
                     forward(6, part).start()
 
-        @pl.when(is_feeder)
-        def _():
-            own_hub[d] = jnp.zeros(own_hub.shape[1:], jnp.float32)
-
-        return lax.cond(i > 0, lambda: finish(i - 1, total), lambda: total)
-
-    total = lax.fori_loop(0, 4, one_step, jnp.zeros((rows, 1), jnp.float32))
+        @pl.when(jnp.logical_and(i >= 1, is_feeder))
+        def _():
+            own_hub[owner(i - 1)] = jnp.zeros(own_hub.shape[1:], jnp.float32)
+
+        return lax.cond(i > 1, lambda: finish(i - 2, total), lambda: total)
+
+    total = lax.fori_loop(0, 5, one_step, jnp.zeros((rows, 1), jnp.float32))
     total = finish(3, total)
 
     width = columns * 4

time: 211 us -> 204 us (0.967)
  Pallas kernels: 208 us -> 201 us
    pallas_call x1, Pallas kernels: 208 us -> 201 us  [local_fused(): pl.pallas_call(fused_kernel, out_shape=jax.ShapeDtypeStruct((rows, width)...]
where the time goes in v5:
time: 204 us
  Pallas kernels  201 us (99%)
  local copies, waits for them, and re-layouts  2.85 us (1%)
    pallas_call x1, Pallas kernels, local_fused(): pl.pallas_call(fused_kernel, out_shape=jax.ShapeDtypeStruct((rows, width)...  201 us

profile of v5, /device:TPU:0, one launch (start us, length us, event | category | flops | bytes accessed | tf_op | source)
XLA Modules:
  0.0 204.1 jit_solution(9868549171634388669)
XLA Ops:
  0.0 201.3 %shard_map.73 = bf16[128,7168]{1,0:T(8,128)(2,1)} custom-call(bf16[128,4096]{1,0:T(8,128)(2,1)} %q_ref.1, bf16[128,4096]{1,0:T(8,128)(2,1)} %k_ref.1, bf16[128,4096]{1,0:T(8,128)(2,1)} %v_ref.1, bf16[512,1792]{1,0:T(8,128)(2,1)} %w_ref.1, bf16[128,7168]{1,0:T(8,128)(2,1)} %res_ref.1, f32[1,7168]{1,0:T(1,128)} %bitcast.2, f32[1,7168]{1,0:T(1,128)} %bitcast.3), custom_call_target="tpu_custom_call" | custom-call | tf_op jit(solution)/shard_map/pallas_call | solution.py:555
  201.3 2.8 %copy.9 = bf16[128,7168]{1,0:T(8,128)(2,1)} copy(bf16[128,7168]{1,0:T(8,128)(2,1)} %shard_map.73) | data formatting | bytes 3670016

commit v6 on v5

--- a/solution.py
+++ b/solution.py
@@ -202,12 +202,13 @@
             def _():
                 forward(h, 0).start()
 
+        if h == 0:
+            @pl.when(is_feeder)
+            def _():
+                feed_w().start()
+
         if h == 1:
             forward(1, 1).start()
-
-            @pl.when(is_feeder)
-            def _():
-                feed_w().start()
 
     for part in range(2):
         keep_w(part).start()
@@ -300,11 +301,11 @@
 
         @pl.when(jnp.logical_and(h == 2, is_hub))
         def _():
-            w_arrive(0, yi, xdp)
-            forward(3, 0).start()
             w_arrive(2, yi, dp)
             forward(0, 2).start()
             forward(2, 2).start()
+            w_arrive(0, yi, xdp)
+            forward(3, 0).start()
 
         return carry
 
@@ -478,9 +479,10 @@
         def _():
             own_hub[owner(i - 1)] = jnp.zeros(own_hub.shape[1:], jnp.float32)
 
-        return lax.cond(i > 1, lambda: finish(i - 2, total), lambda: total)
+        return lax.cond(i > 2, lambda: finish(i - 3, total), lambda: total)
 
     total = lax.fori_loop(0, 5, one_step, jnp.zeros((rows, 1), jnp.float32))
+    total = finish(2, total)
     total = finish(3, total)
 
     width = columns * 4

time: 204 us -> 204 us (level)
  no operation moved by 1% of the time
where the time goes in v6:
time: 204 us
  Pallas kernels  201 us (99%)
  local copies, waits for them, and re-layouts  2.85 us (1%)
    pallas_call x1, Pallas kernels, local_fused(): pl.pallas_call(fused_kernel, out_shape=jax.ShapeDtypeStruct((rows, width)...  201 us

profile of v6, /device:TPU:0, one launch (start us, length us, event | category | flops | bytes accessed | tf_op | source)
XLA Modules:
  0.0 204.1 jit_solution(8858272405697858875)
XLA Ops:
  0.0 201.3 %shard_map.73 = bf16[128,7168]{1,0:T(8,128)(2,1)} custom-call(bf16[128,4096]{1,0:T(8,128)(2,1)} %q_ref.1, bf16[128,4096]{1,0:T(8,128)(2,1)} %k_ref.1, bf16[128,4096]{1,0:T(8,128)(2,1)} %v_ref.1, bf16[512,1792]{1,0:T(8,128)(2,1)} %w_ref.1, bf16[128,7168]{1,0:T(8,128)(2,1)} %res_ref.1, f32[1,7168]{1,0:T(1,128)} %bitcast.2, f32[1,7168]{1,0:T(1,128)} %bitcast.3), custom_call_target="tpu_custom_call" | custom-call | tf_op jit(solution)/shard_map/pallas_call | solution.py:557
  201.3 2.8 %copy.9 = bf16[128,7168]{1,0:T(8,128)(2,1)} copy(bf16[128,7168]{1,0:T(8,128)(2,1)} %shard_map.73) | data formatting | bytes 3670016

commit v7 on v6

--- a/solution.py
+++ b/solution.py
@@ -548,7 +548,7 @@
     hd = queries.shape[1] // HEADS
     heads = group // hd
     length = rows * 8
-    hub_part = columns // 7 * 4
+    hub_part = columns // 7 * 3
     chain_part = columns - hub_part
     bf16, f32 = jnp.bfloat16, jnp.float32
     dma = pltpu.SemaphoreType.DMA

time: 204 us -> 201 us (0.985)
  Pallas kernels: 201 us -> 198 us
    pallas_call x1, Pallas kernels: 201 us -> 198 us  [local_fused(): pl.pallas_call(fused_kernel, out_shape=jax.ShapeDtypeStruct((rows, width)...]
where the time goes in v7:
time: 201 us
  Pallas kernels  198 us (99%)
  local copies, waits for them, and re-layouts  2.85 us (1%)
    pallas_call x1, Pallas kernels, local_fused(): pl.pallas_call(fused_kernel, out_shape=jax.ShapeDtypeStruct((rows, width)...  198 us

profile of v7, /device:TPU:0, one launch (start us, length us, event | category | flops | bytes accessed | tf_op | source)
XLA Modules:
  0.0 201.3 jit_solution(3970487542033040304)
XLA Ops:
  0.0 198.4 %shard_map.73 = bf16[128,7168]{1,0:T(8,128)(2,1)} custom-call(bf16[128,4096]{1,0:T(8,128)(2,1)} %q_ref.1, bf16[128,4096]{1,0:T(8,128)(2,1)} %k_ref.1, bf16[128,4096]{1,0:T(8,128)(2,1)} %v_ref.1, bf16[512,1792]{1,0:T(8,128)(2,1)} %w_ref.1, bf16[128,7168]{1,0:T(8,128)(2,1)} %res_ref.1, f32[1,7168]{1,0:T(1,128)} %bitcast.2, f32[1,7168]{1,0:T(1,128)} %bitcast.3), custom_call_target="tpu_custom_call" | custom-call | tf_op jit(solution)/shard_map/pallas_call | solution.py:557
  198.4 2.8 %copy.9 = bf16[128,7168]{1,0:T(8,128)(2,1)} copy(bf16[128,7168]{1,0:T(8,128)(2,1)} %shard_map.73) | data formatting | bytes 3670016

commit v8 on v7

--- a/solution.py
+++ b/solution.py
@@ -548,7 +548,7 @@
     hd = queries.shape[1] // HEADS
     heads = group // hd
     length = rows * 8
-    hub_part = columns // 7 * 3
+    hub_part = columns // 7 * 2
     chain_part = columns - hub_part
     bf16, f32 = jnp.bfloat16, jnp.float32
     dma = pltpu.SemaphoreType.DMA

time: 201 us -> 204 us (1.015)
  Pallas kernels: 198 us -> 201 us
    pallas_call x1, Pallas kernels: 198 us -> 201 us  [local_fused(): pl.pallas_call(fused_kernel, out_shape=jax.ShapeDtypeStruct((rows, width)...]
where the time goes in v8:
time: 204 us
  Pallas kernels  201 us (99%)
  local copies, waits for them, and re-layouts  2.85 us (1%)
    pallas_call x1, Pallas kernels, local_fused(): pl.pallas_call(fused_kernel, out_shape=jax.ShapeDtypeStruct((rows, width)...  201 us

profile of v8, /device:TPU:0, one launch (start us, length us, event | category | flops | bytes accessed | tf_op | source)
XLA Modules:
  0.0 203.6 jit_solution(1353933816315784753)
XLA Ops:
  0.0 200.8 %shard_map.73 = bf16[128,7168]{1,0:T(8,128)(2,1)} custom-call(bf16[128,4096]{1,0:T(8,128)(2,1)} %q_ref.1, bf16[128,4096]{1,0:T(8,128)(2,1)} %k_ref.1, bf16[128,4096]{1,0:T(8,128)(2,1)} %v_ref.1, bf16[512,1792]{1,0:T(8,128)(2,1)} %w_ref.1, bf16[128,7168]{1,0:T(8,128)(2,1)} %res_ref.1, f32[1,7168]{1,0:T(1,128)} %bitcast.2, f32[1,7168]{1,0:T(1,128)} %bitcast.3), custom_call_target="tpu_custom_call" | custom-call | tf_op jit(solution)/shard_map/pallas_call | solution.py:557
  200.8 2.8 %copy.9 = bf16[128,7168]{1,0:T(8,128)(2,1)} copy(bf16[128,7168]{1,0:T(8,128)(2,1)} %shard_map.73) | data formatting | bytes 3670016
